TPU v7x, 32 devices: a whole 2x2x4 slice. The times are simulated.
32 devices in a mesh: depth: 8 (over z, x), rows: 4 (over y, core).
Axes of the slice: x: 2, y: 2, z: 4, core: 2. Of those that a mesh axis runs over, the one named last changes fastest.
Arguments:
- log_density: float32 [32, 512, 2048], P('depth', 'rows'), may hold values from -6 to 6
Outputs:
- frame: float32 [4, 512, 8, 256], P(None, 'rows', 'depth')
All inputs are finite; a program needn't handle non-finite values.
Results may differ from a plain program's by a relative error of at most 0.00002.
Values sent between devices are 32-bit elements; how exact they have to be, the bound alone decides.
A program may use at most 64 MiB of HBM per device.

v0:
```python
import jax
import jax.numpy as jnp
from jax import lax
from jax.sharding import PartitionSpec as P


def with_halo(shard, sides, width):
    for axis, dim in sides:
        size, length = (lax.axis_size(axis), shard.shape[dim])
        up = [(i, (i + 1) % size) for i in range(size - 1)]
        down = [(j, i) for i, j in up]
        last = lax.slice_in_dim(shard, length - width, length, axis=dim)
        leading = lax.slice_in_dim(shard, 0, width, axis=dim)
        before = lax.ppermute(last, axis, up)
        after = lax.ppermute(leading, axis, down)
        shard = jnp.concatenate([before, shard, after], axis=dim)
    return shard


def shade_slab(padded, extinction, count):

    def advance(carry, index):
        accum_colour, accum_opacity = carry
        planes = lax.dynamic_slice_in_dim(padded, index, 3, 0)
        centre = planes[1, 1:-1, 1:-1]
        grad_z = 0.5 * (planes[2, 1:-1, 1:-1] - planes[0, 1:-1, 1:-1])
        grad_y = 0.5 * (planes[1, 2:, 1:-1] - planes[1, :-2, 1:-1])
        grad_x = 0.5 * (planes[1, 1:-1, 2:] - planes[1, 1:-1, :-2])
        length = jnp.sqrt(grad_z * grad_z + grad_y * grad_y + grad_x * grad_x + 1.0)
        facing = (0.6 * grad_z + 0.48 * grad_y + 0.64 * grad_x) / length
        shading = 0.3 + 0.7 * jnp.abs(facing)
        colour = (
            jnp.stack(
                [
                    jax.nn.sigmoid(2.0 * centre),
                    jnp.exp(-centre * centre),
                    jax.nn.sigmoid(-2.0 * centre),
                ]
            )
            * shading
        )
        opacity = 1.0 - jnp.exp(-extinction * jnp.exp(1.5 * centre))
        weight = (1.0 - accum_opacity) * opacity
        return ((accum_colour + weight * colour, accum_opacity + weight), None)

    height = padded.shape[1] - 2
    width = padded.shape[2] - 2
    start = (jnp.zeros((3, height, width), jnp.float32), jnp.zeros((height, width), jnp.float32))
    (colour_sum, opacity_sum), _ = lax.scan(advance, start, jnp.arange(count, dtype=jnp.int32))
    return jnp.concatenate([colour_sum, opacity_sum[None]], axis=0)


def over_pixels(nearer, farther, channel_axis):
    coverage = lax.slice_in_dim(nearer, 3, 4, axis=channel_axis)
    return nearer + (1.0 - coverage) * farther


def local_image(log_density):
    slices = log_density.shape[0]
    row_count = log_density.shape[1]
    depth_count = lax.axis_size("depth")
    classes = log_density.shape[2] // depth_count
    padded = with_halo(log_density, (("depth", 0), ("rows", 1)), 1)
    padded = jnp.pad(padded, ((0, 0), (0, 0), (1, 1)))
    image = shade_slab(padded, 0.5 / (slices * depth_count), slices)
    return image.reshape(4, row_count, classes, depth_count).transpose(0, 1, 3, 2)


def local(log_density):
    depth_count = lax.axis_size("depth")
    levels = depth_count.bit_length() - 1
    partial_value = local_image(log_density)
    layers = lax.all_to_all(partial_value[None], "depth", split_axis=3, concat_axis=0, tiled=True)
    for level in range(levels):
        paired = layers.reshape((layers.shape[0] // 2, 2) + layers.shape[1:])
        layers = over_pixels(paired[:, 0], paired[:, 1], 1)
    return layers[0]


def solution(mesh):
    placed = (P("depth", "rows", None),)
    return jax.shard_map(
        local, mesh=mesh, in_specs=placed, out_specs=P(None, "rows", "depth", None), check_vma=False
    )
```

profile of v0, /device:TPU:0, one launch (start us, length us, event | category | flops | bytes accessed | tf_op | source)
XLA Modules:
  0.0 248.2 jit_solution(3961588044752766542)
XLA Ops:
  0.0 1.9 fusion.10
  1.9 5.0 %collective-permute-start = (f32[1,128,2048]{2,1,0:T(8,128)S(1)}, f32[1,128,2048]{2,1,0:T(8,128)S(1)}, u32[]{:S(2)}, u32[]{:S(2)}) collective-permute-start(f32[1,128,2048]{2,1,0:T(8,128)S(1)} %get-tuple-element.115), channel_id=1, source_target_pairs={{0,4},{4,8},{8,12},{12,16},{16,20},{20,24},{24,28},{1,5},{5,9},{9,... | collective-permute-start | bytes 3145736 | tf_op jit(solution)/shard_map/ppermute | solution.py:14
  6.9 1.3 collective-permute-start.1
  8.2 43.5 %collective-permute-done = f32[1,128,2048]{2,1,0:T(8,128)S(1)} collective-permute-done((f32[1,128,2048]{2,1,0:T(8,128)S(1)}, f32[1,128,2048]{2,1,0:T(8,128)S(1)}, u32[]{:S(2)}, u32[]{:S(2)}) %collective-permute-start) | collective-permute-done | bytes 1048608 | tf_op jit(solution)/shard_map/ppermute | solution.py:14
  51.7 0.1 constant_dynamic-update-slice_fusion.2
  51.8 0.5 constant_dynamic-update-slice_fusion.1
  52.3 0.0 collective-permute-done.1
  52.3 0.1 constant_dynamic-update-slice_fusion
  52.4 2.7 %copy-done.1 = f32[6,128,2048]{2,1,0:T(8,128)} copy-done((f32[6,128,2048]{2,1,0:T(8,128)}, f32[6,128,2048]{2,1,0:T(8,128)S(1)}, u32[]{:S(2)}) %copy-start.1) | copy-done | bytes 6291480
  55.1 0.1 fusion.9
  55.2 1.3 collective-permute-start.2
  56.5 1.3 collective-permute-start.3
  57.8 0.0 collective-permute-done.2
  57.8 3.5 %collective-permute-done.3 = f32[6,1,2048]{2,1,0:T(1,128)S(1)} collective-permute-done((f32[6,1,2048]{2,1,0:T(1,128)S(1)}, f32[6,1,2048]{2,1,0:T(1,128)S(1)}, u32[]{:S(2)}, u32[]{:S(2)}) %collective-permute-start.3) | collective-permute-done | bytes 49184 | tf_op jit(solution)/shard_map/ppermute | solution.py:15
  61.3 6.8 %select_maximum_fusion = f32[6,130,2050]{2,1,0:T(8,128)} fusion(f32[6,1,2048]{2,1,0:T(1,128)S(1)} %collective-permute-done.3, f32[6,128,2048]{2,1,0:T(8,128)} %copy-done.1, f32[6,1,2048]{2,1,0:T(1,128)S(1)} %collective-permute-done.2), kind=kLoop, calls=%fused_computation.15 | loop fusion | flops 12792000 | bytes 12785760 | tf_op jit(solution)/shard_map/concatenate | solution.py:16
  68.2 51.6 %while.15 = (s32[]{:T(128)}, f32[3,128,2048]{2,1,0:T(8,128)S(1)}, f32[128,2048]{1,0:T(8,128)}, s32[4]{0:T(128)S(1)}, f32[6,130,2050]{2,1,0:T(8,128)}, /*index=5*/s32[]{:T(128)}, s32[]{:T(128)}, s32[]{:T(128)}, s32[]{}, s32[]{}) while((s32[]{:T(128)}, f32[3,128,2048]{2,1,0:T(8,128)S(1)}, f32[128,2048]{1,0:T(8,128)}, ...), condition=%wide.region_1.2_spmd.clone, body=%wide.region_0.1_spmd.clone.sunk | while | flops 14680074 | bytes 27263216 | solution.py:49
  68.2 0.6 dynamic_slice.16
  70.6 2.8 %select_add_fusion.2 = (f32[128,2048]{1,0:T(8,128)}, f32[128,2048]{1,0:T(8,128)S(1)}) fusion(f32[128,2048]{1,0:T(8,128)} %get-tuple-element.171, pred[]{:T(512)S(6)} %compare.18, f32[6,130,2050]{2,1,0:T(8,128)} %get-tuple-element.183, s32[]{:T(128)S(6)} %add.188, s32[]{:T(128)S(6)} %add.189), kind=kLoop, calls=%fused_computation.12.clone.1 | loop fusion | flops 1835008 | bytes 4194313 | tf_op jit(solution)/shard_map/while/body/eval_jaxpr/add | solution.py:44
  73.4 5.8 %add_bitcast_fusion.2 = (f32[128,2048]{1,0:T(8,128)S(1)}, f32[1,128,2048]{2,1,0:T(8,128)S(1)}, f32[1,128,2048]{2,1,0:T(8,128)S(1)}, f32[1,128,2048]{2,1,0:T(8,128)S(1)}) fusion(f32[6,130,2050]{2,1,0:T(8,128)} %get-tuple-element.183, s32[]{:T(128)S(6)} %add.188, s32[]{:T(128)S(6)} %add.189, s32[]{:T(128)S(6)} %add.190, s32[]{:T(128)S(6)} %select_n.8, ...), kind=kLoop, calls=%fused_computation.9.clone.1 | loop fusion | flops 8126464 | bytes 11534356 | tf_op jit(solution)/shard_map/while/body/eval_jaxpr/mul | solution.py:33
  79.2 1.6 fusion.12
  80.8 0.6 dynamic_slice.16
  83.3 3.1 %select_add_fusion.2 = (f32[128,2048]{1,0:T(8,128)}, f32[128,2048]{1,0:T(8,128)S(1)}) fusion(f32[128,2048]{1,0:T(8,128)} %get-tuple-element.171, pred[]{:T(512)S(6)} %compare.18, f32[6,130,2050]{2,1,0:T(8,128)} %get-tuple-element.183, s32[]{:T(128)S(6)} %add.188, s32[]{:T(128)S(6)} %add.189), kind=kLoop, calls=%fused_computation.12.clone.1 | loop fusion | flops 1835008 | bytes 4194313 | tf_op jit(solution)/shard_map/while/body/eval_jaxpr/add | solution.py:44
  86.3 5.8 %add_bitcast_fusion.2 = (f32[128,2048]{1,0:T(8,128)S(1)}, f32[1,128,2048]{2,1,0:T(8,128)S(1)}, f32[1,128,2048]{2,1,0:T(8,128)S(1)}, f32[1,128,2048]{2,1,0:T(8,128)S(1)}) fusion(f32[6,130,2050]{2,1,0:T(8,128)} %get-tuple-element.183, s32[]{:T(128)S(6)} %add.188, s32[]{:T(128)S(6)} %add.189, s32[]{:T(128)S(6)} %add.190, s32[]{:T(128)S(6)} %select_n.8, ...), kind=kLoop, calls=%fused_computation.9.clone.1 | loop fusion | flops 8126464 | bytes 11534356 | tf_op jit(solution)/shard_map/while/body/eval_jaxpr/mul | solution.py:33
  92.2 1.6 fusion.12
  93.8 0.6 dynamic_slice.16
  96.3 3.1 %select_add_fusion.2 = (f32[128,2048]{1,0:T(8,128)}, f32[128,2048]{1,0:T(8,128)S(1)}) fusion(f32[128,2048]{1,0:T(8,128)} %get-tuple-element.171, pred[]{:T(512)S(6)} %compare.18, f32[6,130,2050]{2,1,0:T(8,128)} %get-tuple-element.183, s32[]{:T(128)S(6)} %add.188, s32[]{:T(128)S(6)} %add.189), kind=kLoop, calls=%fused_computation.12.clone.1 | loop fusion | flops 1835008 | bytes 4194313 | tf_op jit(solution)/shard_map/while/body/eval_jaxpr/add | solution.py:44
  99.4 5.7 %add_bitcast_fusion.2 = (f32[128,2048]{1,0:T(8,128)S(1)}, f32[1,128,2048]{2,1,0:T(8,128)S(1)}, f32[1,128,2048]{2,1,0:T(8,128)S(1)}, f32[1,128,2048]{2,1,0:T(8,128)S(1)}) fusion(f32[6,130,2050]{2,1,0:T(8,128)} %get-tuple-element.183, s32[]{:T(128)S(6)} %add.188, s32[]{:T(128)S(6)} %add.189, s32[]{:T(128)S(6)} %add.190, s32[]{:T(128)S(6)} %select_n.8, ...), kind=kLoop, calls=%fused_computation.9.clone.1 | loop fusion | flops 8126464 | bytes 11534356 | tf_op jit(solution)/shard_map/while/body/eval_jaxpr/mul | solution.py:33
  105.1 1.6 fusion.12
  106.7 0.6 dynamic_slice.16
  109.2 3.1 %select_add_fusion.2 = (f32[128,2048]{1,0:T(8,128)}, f32[128,2048]{1,0:T(8,128)S(1)}) fusion(f32[128,2048]{1,0:T(8,128)} %get-tuple-element.171, pred[]{:T(512)S(6)} %compare.18, f32[6,130,2050]{2,1,0:T(8,128)} %get-tuple-element.183, s32[]{:T(128)S(6)} %add.188, s32[]{:T(128)S(6)} %add.189), kind=kLoop, calls=%fused_computation.12.clone.1 | loop fusion | flops 1835008 | bytes 4194313 | tf_op jit(solution)/shard_map/while/body/eval_jaxpr/add | solution.py:44
  112.3 5.9 %add_bitcast_fusion.2 = (f32[128,2048]{1,0:T(8,128)S(1)}, f32[1,128,2048]{2,1,0:T(8,128)S(1)}, f32[1,128,2048]{2,1,0:T(8,128)S(1)}, f32[1,128,2048]{2,1,0:T(8,128)S(1)}) fusion(f32[6,130,2050]{2,1,0:T(8,128)} %get-tuple-element.183, s32[]{:T(128)S(6)} %add.188, s32[]{:T(128)S(6)} %add.189, s32[]{:T(128)S(6)} %add.190, s32[]{:T(128)S(6)} %select_n.8, ...), kind=kLoop, calls=%fused_computation.9.clone.1 | loop fusion | flops 8126464 | bytes 11534356 | tf_op jit(solution)/shard_map/while/body/eval_jaxpr/mul | solution.py:33
  118.2 1.6 fusion.12
  119.8 2.6 %copy.9 = f32[128,2048]{0,1:T(8,128)} copy(f32[128,2048]{1,0:T(8,128)} %get-tuple-element.74) | data formatting | bytes 2097152 | tf_op jit(solution)/shard_map/while | solution.py:49
  122.4 2.3 copy.8
  124.7 2.5 %maximum_bitcast_fusion = f32[1,4,128,8,256]{2,3,4,1,0:T(8,128)S(1)} fusion(f32[1,128,256,8]{1,3,2,0:T(8,128)} %bitcast.62, f32[3,128,256,8]{1,3,2,0:T(8,128)} %bitcast.59), kind=kLoop, calls=%fused_computation.18 | loop fusion | flops 1048576 | bytes 8388608 | tf_op jit(solution)/shard_map/broadcast_in_dim | solution.py:73
  127.2 0.8 copy.10
  128.1 99.1 %all_to_all.15 = f32[1,4,128,8,256]{2,4,1,0,3:T(8,128)S(1)} all-to-all(f32[1,4,128,8,256]{2,4,1,0,3:T(8,128)S(1)} %copy.10), channel_id=1, replica_groups=mesh['depth'=8,'rows'=4] {'depth'}, dimensions={3} | all-to-all | bytes 8388608 | tf_op jit(solution)/shard_map/all_to_all | solution.py:73
  227.2 1.9 slice_bitcast_fusion.4
  229.2 0.2 copy.12
  229.4 6.0 %copy.13 = f32[4,1,4,128,1,256]{5,4,3,2,1,0:T(1,128)} copy(f32[4,1,4,128,1,256]{3,5,2,1,0,4:T(8,128)} %get-tuple-element.112) | data formatting | bytes 4194304 | tf_op jit(solution)/shard_map/slice | solution.py:76
  235.4 3.6 %copy.11 = f32[4,1,4,128,1,256]{5,4,3,2,1,0:T(1,128)} copy(f32[4,1,4,128,1,256]{3,5,2,1,0,4:T(8,128)S(1)} %get-tuple-element.113) | data formatting | bytes 4194304 | tf_op jit(solution)/shard_map/slice | solution.py:76
  239.0 5.0 %fusion.4 = f32[2,2,4,128,1,256]{5,4,3,2,1,0:T(1,128)S(1)} fusion(f32[2,2,128,256]{3,2,1,0:T(8,128)S(1)} %copy.12, f32[2,2,4,128,1,256]{5,4,3,2,1,0:T(1,128)} %bitcast.60, f32[2,2,4,128,1,256]{5,4,3,2,1,0:T(1,128)} %bitcast.61), kind=kLoop, calls=%fused_computation.20 | loop fusion | flops 1048576 | bytes 6815744 | tf_op jit(solution)/shard_map/add | solution.py:55
  244.1 0.7 slice_bitcast_fusion.1
  244.8 0.3 slice_subtract_fusion.1
  245.1 1.2 fusion.6
  246.3 0.4 slice_bitcast_fusion.3
  246.7 0.1 slice_subtract_fusion.2
  246.8 1.4 fusion.8
  (9 shorter events, 0.1 us)
Async XLA Ops:
  0.0 51.8 %copy-start = (f32[4,128,2048]{2,1,0:T(8,128)S(1)}, f32[4,128,2048]{2,1,0:T(8,128)}, u32[]{:S(2)}) copy-start(f32[4,128,2048]{2,1,0:T(8,128)} %param.3) | copy-start | bytes 12582916
  1.9 49.9 %collective-permute-start = (f32[1,128,2048]{2,1,0:T(8,128)S(1)}, f32[1,128,2048]{2,1,0:T(8,128)S(1)}, u32[]{:S(2)}, u32[]{:S(2)}) collective-permute-start(f32[1,128,2048]{2,1,0:T(8,128)S(1)} %get-tuple-element.115), channel_id=1, source_target_pairs={{0,4},{4,8},{8,12},{12,16},{16,20},{20,24},{24,28},{1,5},{5,9},{9,... | collective-permute-start | bytes 3145736 | tf_op jit(solution)/shard_map/ppermute | solution.py:14
  6.9 45.4 %collective-permute-start.1 = (f32[1,128,2048]{2,1,0:T(8,128)S(1)}, f32[1,128,2048]{2,1,0:T(8,128)S(1)}, u32[]{:S(2)}, u32[]{:S(2)}) collective-permute-start(f32[1,128,2048]{2,1,0:T(8,128)S(1)} %get-tuple-element.114), channel_id=1, source_target_pairs={{4,0},{8,4},{12,8},{16,12},{20,16},{24,20},{28,24},{5,1},{9,5},{13... | collective-permute-start | bytes 3145736 | tf_op jit(solution)/shard_map/ppermute | solution.py:15
  52.4 2.7 %copy-start.1 = (f32[6,128,2048]{2,1,0:T(8,128)}, f32[6,128,2048]{2,1,0:T(8,128)S(1)}, u32[]{:S(2)}) copy-start(f32[6,128,2048]{2,1,0:T(8,128)S(1)} %constant_dynamic-update-slice_fusion) | copy-start | bytes 18874372
  55.2 2.6 %collective-permute-start.2 = (f32[6,1,2048]{2,1,0:T(1,128)S(1)}, f32[6,1,2048]{2,1,0:T(1,128)S(1)}, u32[]{:S(2)}, u32[]{:S(2)}) collective-permute-start(f32[6,1,2048]{2,1,0:T(1,128)S(1)} %get-tuple-element.109), channel_id=1, source_target_pairs={{0,1},{1,2},{2,3},{4,5},{5,6},{6,7},{8,9},{9,10},{10,11},{12,13},{... | collective-permute-start | bytes 147464 | tf_op jit(solution)/shard_map/ppermute | solution.py:14
  56.5 4.9 %collective-permute-start.3 = (f32[6,1,2048]{2,1,0:T(1,128)S(1)}, f32[6,1,2048]{2,1,0:T(1,128)S(1)}, u32[]{:S(2)}, u32[]{:S(2)}) collective-permute-start(f32[6,1,2048]{2,1,0:T(1,128)S(1)} %get-tuple-element.110), channel_id=1, source_target_pairs={{1,0},{2,1},{3,2},{5,4},{6,5},{7,6},{9,8},{10,9},{11,10},{13,12},{... | collective-permute-start | bytes 147464 | tf_op jit(solution)/shard_map/ppermute | solution.py:15
where the time goes:
time: 250 us; the launch traced here: 248 us
  blocking collectives  99.1 us (40%)
  other arithmetic  59.1 us (24%)
  waiting for transfers between devices  47.1 us (19%)
  local copies, waits for them, and re-layouts  26.2 us (10%)
  starting transfers between devices  8.92 us (4%)
  loops' own time  7.52 us (3%)
    all_to_all x1, blocking collectives, local(): lax.all_to_all(partial_value[None], 'depth', split_axis=3, concat_axis=0,...  99.1 us
    ppermute x2, waiting for transfers between devices, with_halo(): before = lax.ppermute(last, axis, up)  43.5 us
    mul x4, other arithmetic, advance(): jnp.stack([jax.nn.sigmoid(2.0 * centre), jnp.exp(-centre * centre), jax.n...  23.2 us
    add x8, other arithmetic, advance(): return ((accum_colour + weight * colour, accum_opacity + weight), None)  18.5 us
    slice x2, local copies, waits for them, and re-layouts, local(): layers = over_pixels(paired[:, 0], paired[:, 1], 1)  9.66 us
    add x3, other arithmetic, over_pixels(): return nearer + (1.0 - coverage) * farther  7.61 us
    another operation x1, loops' own time, shade_slab(): lax.scan(advance, start, jnp.arange(count, dtype=jnp.int32))  7.52 us
    concatenate x1, other arithmetic, with_halo(): shard = jnp.concatenate([before, shard, after], axis=dim)  6.83 us
  transfers between devices with their start and end apart: 4, of which 2 were waited for; matrix products, arithmetic and copies ran while one was open for 0% of the time, Pallas kernels for 0%

commit v1 on v0

--- a/solution.py
+++ b/solution.py
@@ -1,7 +1,16 @@
+import functools
+
 import jax
 import jax.numpy as jnp
 from jax import lax
+from jax.experimental import pallas as pl
+from jax.experimental.pallas import tpu as pltpu
 from jax.sharding import PartitionSpec as P
+
+MESH = pl.DeviceIdType.MESH
+TILE = 8
+LANES = 128
+BLOCK = 256
 
 
 def with_halo(shard, sides, width):
@@ -55,26 +64,347 @@
     return nearer + (1.0 - coverage) * farther
 
 
-def local_image(log_density):
-    slices = log_density.shape[0]
-    row_count = log_density.shape[1]
+def local_general(log_density):
+    slices, row_count, width = log_density.shape
     depth_count = lax.axis_size("depth")
-    classes = log_density.shape[2] // depth_count
+    classes = width // depth_count
     padded = with_halo(log_density, (("depth", 0), ("rows", 1)), 1)
     padded = jnp.pad(padded, ((0, 0), (0, 0), (1, 1)))
     image = shade_slab(padded, 0.5 / (slices * depth_count), slices)
-    return image.reshape(4, row_count, classes, depth_count).transpose(0, 1, 3, 2)
-
-
-def local(log_density):
-    depth_count = lax.axis_size("depth")
-    levels = depth_count.bit_length() - 1
-    partial_value = local_image(log_density)
+    partial_value = image.reshape(4, row_count, classes, depth_count).transpose(0, 1, 3, 2)
     layers = lax.all_to_all(partial_value[None], "depth", split_axis=3, concat_axis=0, tiled=True)
-    for level in range(levels):
+    while layers.shape[0] > 1:
         paired = layers.reshape((layers.shape[0] // 2, 2) + layers.shape[1:])
         layers = over_pixels(paired[:, 0], paired[:, 1], 1)
     return layers[0]
+
+
+def bit_reversed(value, bits):
+    return sum(((value >> b) & 1) << (bits - 1 - b) for b in range(bits))
+
+
+def kernel(depth, rows, vol_ref, edge_ref, out_ref, cells, edges, spread, image, *rest):
+    S, tiles, _, W = vol_ref.shape
+    chunks = tiles // 2
+    groups = depth // 2
+    steps = groups.bit_length() - 1
+    part = LANES * depth
+    span = pl.ds(LANES, W)
+    extinction = 0.5 / (S * depth)
+
+    held, came = rest[: steps + 1], rest[steps + 1 : 2 * steps + 1]
+    (own_sem, own_edge_sem, pair_send, pair_recv, edge_send, edge_recv, row_send, row_recv,
+     face_send, face_recv, part_send, part_recv, last_send, last_recv) = rest[2 * steps + 1 :]
+
+    me, row = lax.axis_index("depth"), lax.axis_index("rows")
+    x, z = lax.rem(me, 2), me // 2
+    first = me - x
+    partner = first + 1 - x
+    mine = 1 + S * x
+
+    near = [(partner, row, None)]
+    offsets = [(-1, z >= 1), (1, z <= groups - 2)]
+    for d, there in offsets:
+        near.append((me + 2 * d, row, there))
+    for k in range(1, steps):
+        near.append((2 * (z + (1 << k) * (1 - 2 * (lax.rem(z // (1 << k), 2)))) + x, row, None))
+    for d, there in ((-1, row >= 1), (1, row <= rows - 2)):
+        near.append((first, row + d, there))
+        near.append((first + 1, row + d, there))
+    barrier = pltpu.get_barrier_semaphore()
+    count = 0
+    for dd, rr, there in near:
+        def greet(dd=dd, rr=rr):
+            pl.semaphore_signal(barrier, inc=1, device_id=(dd, rr), device_id_type=MESH)
+        if there is None:
+            greet()
+            count = count + 1
+        else:
+            pl.when(there)(greet)
+            count = count + there.astype(jnp.int32)
+
+    own = pltpu.make_async_copy(
+        vol_ref.at[:, pl.ds(x * chunks, chunks)],
+        cells.at[pl.ds(mine, S), pl.ds(1, chunks), :, span],
+        own_sem,
+    )
+    own.start()
+    own_edge = pltpu.make_async_copy(edge_ref.at[2 - x], edges.at[1 - x, x], own_edge_sem)
+    own_edge.start()
+    pl.semaphore_wait(barrier, count)
+
+    def pair_copy(c):
+        return pltpu.make_async_remote_copy(
+            src_ref=vol_ref.at[:, (1 - x) * chunks + c],
+            dst_ref=cells.at[pl.ds(mine, S), 1 + c, :, span],
+            send_sem=pair_send.at[c], recv_sem=pair_recv.at[c],
+            device_id=(partner, row), device_id_type=MESH,
+        )
+
+    def edge_copy():
+        return pltpu.make_async_remote_copy(
+            src_ref=edge_ref.at[1 + x], dst_ref=edges.at[x, x],
+            send_sem=edge_send, recv_sem=edge_recv,
+            device_id=(partner, row), device_id_type=MESH,
+        )
+
+    def row_copy(direction):
+        return pltpu.make_async_remote_copy(
+            src_ref=edge_ref.at[3 - 3 * direction], dst_ref=edges.at[direction, x],
+            send_sem=row_send.at[direction], recv_sem=row_recv.at[x],
+            device_id=(first + direction, row + 1 - 2 * direction), device_id_type=MESH,
+        )
+
+    def row_arrival(source):
+        return pltpu.make_async_remote_copy(
+            src_ref=edge_ref.at[0], dst_ref=edges.at[x, source],
+            send_sem=row_send.at[0], recv_sem=row_recv.at[source],
+            device_id=(partner, row), device_id_type=MESH,
+        )
+
+    def face_copy(direction, c):
+        return pltpu.make_async_remote_copy(
+            src_ref=cells.at[2 * S if direction == 0 else 1, 1 + c, :, span],
+            dst_ref=cells.at[0 if direction == 0 else 2 * S + 1, 1 + c, :, span],
+            send_sem=face_send.at[direction, c], recv_sem=face_recv.at[direction, c],
+            device_id=(me + (2 if direction == 0 else -2), row), device_id_type=MESH,
+        )
+
+    def part_copy(k, c):
+        half = groups >> (k + 1)
+        bit = lax.rem(z // (1 << k), 2)
+        return pltpu.make_async_remote_copy(
+            src_ref=held[k].at[c, pl.ds((1 - bit) * half, half)], dst_ref=came[k].at[c],
+            send_sem=part_send.at[k, c], recv_sem=part_recv.at[k, c],
+            device_id=(me + 2 * (1 << k) * (1 - 2 * bit), row), device_id_type=MESH,
+        )
+
+    def last_copy(c):
+        return pltpu.make_async_remote_copy(
+            src_ref=held[steps].at[c, 0, 1 - x], dst_ref=out_ref.at[:, x * chunks + c],
+            send_sem=last_send.at[c], recv_sem=last_recv.at[c],
+            device_id=(partner, row), device_id_type=MESH,
+        )
+
+    edge_copy().start()
+
+    @pl.loop(0, chunks)
+    def _(c):
+        pair_copy(c).start()
+
+    has_next_row, has_prev_row = row <= rows - 2, row >= 1
+    has_next, has_prev = z <= groups - 2, z >= 1
+    has_edge = jnp.logical_or(jnp.logical_and(x == 0, has_prev_row), jnp.logical_and(x == 1, has_next_row))
+    pl.when(has_next_row)(lambda: row_copy(0).start())
+    pl.when(has_prev_row)(lambda: row_copy(1).start())
+
+    @pl.loop(0, 2 * S + 2)
+    def _(s):
+        cells[s, :, :, 0:LANES] = jnp.zeros((chunks + 2, TILE, LANES), jnp.float32)
+        cells[s, :, :, LANES + W :] = jnp.zeros((chunks + 2, TILE, LANES), jnp.float32)
+
+    @pl.when(jnp.logical_not(has_prev))
+    def _():
+        @pl.loop(0, chunks)
+        def _(c):
+            cells[0, 1 + c, :, span] = jnp.zeros((TILE, W), jnp.float32)
+
+    @pl.when(jnp.logical_not(has_next))
+    def _():
+        @pl.loop(0, chunks)
+        def _(c):
+            cells[2 * S + 1, 1 + c, :, span] = jnp.zeros((TILE, W), jnp.float32)
+
+    @pl.loop(0, part // 16)
+    def _(b):
+        at = lax.broadcasted_iota(jnp.int32, (16, part), 0) + b * 16
+        to = lax.broadcasted_iota(jnp.int32, (16, part), 1)
+        source = (to % LANES) * depth + to // LANES
+        spread[pl.ds(pl.multiple_of(b * 16, 16), 16), :] = jnp.where(at == source, 1.0, 0.0).astype(jnp.bfloat16)
+
+    own.wait()
+    own_edge.wait()
+    edge_copy().wait()
+    pl.when(has_next_row)(lambda: row_copy(0).wait_send())
+    pl.when(has_prev_row)(lambda: row_copy(1).wait_send())
+
+    @pl.when(has_edge)
+    def _():
+        row_arrival(0).wait_recv()
+        row_arrival(1).wait_recv()
+
+    @pl.when(jnp.logical_not(has_edge))
+    def _():
+        edges[x] = jnp.zeros(edges.shape[1:], jnp.float32)
+
+    for s in range(2 * S):
+        cells[1 + s, 0, TILE - 1 : TILE, LANES : LANES + W] = edges[0, s // S, s % S : s % S + 1, :]
+        cells[1 + s, chunks + 1, 0:1, LANES : LANES + W] = edges[1, s // S, s % S : s % S + 1, :]
+
+    row_of = lax.broadcasted_iota(jnp.int32, (TILE, BLOCK), 0)
+    is_top, is_bottom = row_of == 0, row_of == TILE - 1
+
+    def shade(c):
+        t = 1 + c
+
+        def columns(b, carry):
+            base = pl.multiple_of(b * BLOCK, BLOCK)
+            mid = pl.ds(pl.multiple_of(base + LANES, LANES), BLOCK)
+            red = green = blue = alpha = jnp.zeros((TILE, BLOCK), jnp.float32)
+            before = cells[0, t, :, mid]
+            wide = cells[1, t, :, pl.ds(base, BLOCK + 2 * LANES)]
+            for s in range(1, 2 * S + 1):
+                centre = wide[:, LANES : LANES + BLOCK]
+                if s < 2 * S:
+                    wide_after = cells[s + 1, t, :, pl.ds(base, BLOCK + 2 * LANES)]
+                    after = wide_after[:, LANES : LANES + BLOCK]
+                else:
+                    wide_after, after = None, cells[s + 1, t, :, mid]
+                left = pltpu.roll(wide, 1, 1)[:, LANES : LANES + BLOCK]
+                right = pltpu.roll(wide, BLOCK + 2 * LANES - 1, 1)[:, LANES : LANES + BLOCK]
+                above = jnp.where(is_top, cells[s, t - 1, TILE - 1 : TILE, mid], pltpu.roll(centre, 1, 0))
+                below = jnp.where(is_bottom, cells[s, t + 1, 0:1, mid], pltpu.roll(centre, TILE - 1, 0))
+                dz, dy, dx = after - before, below - above, right - left
+                square = dz * dz + dy * dy + dx * dx + 4.0
+                facing = 0.42 * dz + 0.336 * dy + 0.448 * dx
+                shading = 0.3 + jnp.abs(facing) * lax.rsqrt(square)
+                opacity = 1.0 - jnp.exp(-extinction * jnp.exp(1.5 * centre))
+                weight = (1.0 - alpha) * opacity
+                lit = weight * shading
+                half = 0.5 * lit
+                swing = half * jnp.tanh(centre)
+                red = red + (half + swing)
+                green = green + lit * jnp.exp(-centre * centre)
+                blue = blue + (half - swing)
+                alpha = alpha + weight
+                before, wide = centre, wide_after
+            for ch, value in enumerate((red, green, blue, alpha)):
+                image[ch, :, pl.ds(base, BLOCK)] = value
+            return carry
+
+        lax.fori_loop(0, W // BLOCK, columns, 0)
+        for g in range(W // part):
+            piece = image[:, :, g * part : (g + 1) * part].reshape(4 * TILE, part)
+            high = piece.astype(jnp.bfloat16)
+            low = (piece - high.astype(jnp.float32)).astype(jnp.bfloat16)
+            both = jnp.dot(
+                jnp.concatenate([high, low], axis=0), spread[...], preferred_element_type=jnp.float32
+            )
+            sorted_ = both[: 4 * TILE] + both[4 * TILE :]
+            for j in range(depth):
+                place = bit_reversed(j // 2, steps)
+                held[0][c, place, j % 2, :, :, g * LANES : (g + 1) * LANES] = sorted_[
+                    :, j * LANES : (j + 1) * LANES
+                ].reshape(4, TILE, LANES)
+
+    def combine(k, c):
+        half = groups >> (k + 1)
+        bit = lax.rem(z // (1 << k), 2)
+        copy = part_copy(k, c)
+        copy.wait_recv()
+
+        def join(near_of, far_of):
+            for i in range(half):
+                for p in range(2):
+                    near, far = near_of(i, p), far_of(i, p)
+                    clear = 1.0 - near[3]
+                    for ch in range(4):
+                        held[k + 1][c, i, p, ch] = near[ch] + clear * far[ch]
+
+        def kept(i, p):
+            return held[k][c, bit * half + i, p]
+
+        def received(i, p):
+            return came[k][c, i, p]
+
+        pl.when(bit == 0)(lambda: join(kept, received))
+        pl.when(bit == 1)(lambda: join(received, kept))
+
+    @pl.loop(0, chunks + steps + 1)
+    def _(i):
+        @pl.when(i < chunks)
+        def _():
+            pair_copy(i).wait_recv()
+            pl.when(has_next)(lambda: face_copy(0, i).start())
+            pl.when(has_prev)(lambda: face_copy(1, i).start())
+
+        @pl.when(jnp.logical_and(i >= 1, i <= chunks))
+        def _():
+            c = i - 1
+            pl.when(has_prev)(lambda: face_copy(0, c).wait_recv())
+            pl.when(has_next)(lambda: face_copy(1, c).wait_recv())
+            shade(c)
+            part_copy(0, c).start()
+
+        for k in range(steps):
+
+            @pl.when(jnp.logical_and(i >= k + 2, i <= chunks + k + 1))
+            def _(k=k):
+                c = i - 2 - k
+                combine(k, c)
+                if k + 1 < steps:
+                    part_copy(k + 1, c).start()
+                else:
+                    out_ref[:, x * chunks + c] = held[steps][c, 0, x]
+                    last_copy(c).start()
+
+    @pl.loop(0, chunks)
+    def _(c):
+        pair_copy(c).wait_send()
+        pl.when(has_next)(lambda: face_copy(0, c).wait_send())
+        pl.when(has_prev)(lambda: face_copy(1, c).wait_send())
+        for k in range(steps):
+            part_copy(k, c).wait_send()
+        last_copy(c).wait()
+
+
+def local(log_density):
+    S, R, W = log_density.shape
+    depth, rows = lax.axis_size("depth"), lax.axis_size("rows")
+    groups = depth // 2
+    fits = (
+        depth >= 4
+        and depth & (depth - 1) == 0
+        and W % (LANES * depth) == 0
+        and W % BLOCK == 0
+        and R % (2 * TILE) == 0
+    )
+    if not fits:
+        return local_general(log_density)
+    steps = groups.bit_length() - 1
+    tiles = R // TILE
+    chunks = tiles // 2
+    Cw = W // depth
+    edge_rows = jnp.stack([log_density[:, r] for r in (0, R // 2 - 1, R // 2, R - 1)])
+    F32 = jnp.float32
+    parts = [pltpu.VMEM((chunks, groups >> k, 2, 4, TILE, Cw), F32) for k in range(steps + 1)]
+    arrivals = [pltpu.VMEM((chunks, groups >> (k + 1), 2, 4, TILE, Cw), F32) for k in range(steps)]
+    DMA = pltpu.SemaphoreType.DMA
+    out = pl.pallas_call(
+        functools.partial(kernel, depth, rows),
+        out_shape=jax.ShapeDtypeStruct((4, tiles, TILE, Cw), F32),
+        in_specs=[pl.BlockSpec(memory_space=pl.ANY)] * 2,
+        out_specs=pl.BlockSpec(memory_space=pltpu.VMEM),
+        scratch_shapes=[
+            pltpu.VMEM((2 * S + 2, chunks + 2, TILE, W + 2 * LANES), F32),
+            pltpu.VMEM((2, 2, S, W), F32),
+            pltpu.VMEM((LANES * depth, LANES * depth), jnp.bfloat16),
+            pltpu.VMEM((4, TILE, W), F32),
+            *parts,
+            *arrivals,
+            DMA, DMA,
+            DMA((chunks,)), DMA((chunks,)),
+            DMA, DMA,
+            DMA((2,)), DMA((2,)),
+            DMA((2, chunks)), DMA((2, chunks)),
+            DMA((steps, chunks)), DMA((steps, chunks)),
+            DMA((chunks,)), DMA((chunks,)),
+        ],
+        compiler_params=pltpu.CompilerParams(
+            collective_id=0, has_side_effects=True, vmem_limit_bytes=40 * 1024 * 1024
+        ),
+    )(log_density.reshape(S, tiles, TILE, W), edge_rows)
+    return out.reshape(4, R, 1, Cw)
 
 
 def solution(mesh):

time: 250 us -> 116 us (0.46)
  Pallas kernels: 0 us -> 111 us
  blocking collectives: 99.1 us -> 0 us
  other arithmetic: 59.1 us -> 0.03 us
  waiting for transfers between devices: 47.1 us -> 0 us
  local copies, waits for them, and re-layouts: 26.2 us -> 4.85 us
  starting transfers between devices: 8.92 us -> 0 us
  loops' own time: 7.52 us -> 0 us
    pallas_call x0 -> x1, Pallas kernels: none -> 111 us  [local(): pl.pallas_call(functools.partial(kernel, depth, rows), out_shape=jax.Shap...]
    all_to_all x1 -> x0, blocking collectives: 99.1 us -> none  [local(): lax.all_to_all(partial_value[None], 'depth', split_axis=3, concat_axis=0,...]
    ppermute x4 -> x0, waiting for transfers between devices: 47.1 us -> none  [the longest x2 43.5 us: with_halo(): before = lax.ppermute(last, axis, up)]
    add x11 -> x0, other arithmetic: 26.1 us -> none  [the longest x8 18.5 us: advance(): return ((accum_colour + weight * colour, accum_opacity + weight), None)]
    mul x4 -> x0, other arithmetic: 23.2 us -> none  [advance(): jnp.stack([jax.nn.sigmoid(2.0 * centre), jnp.exp(-centre * centre), jax.n...]
    slice x4 -> x1, local copies, waits for them, and re-layouts: 11.6 us -> 1.28 us  [local(): log_density[:, r]]
    ppermute x4 -> x0, starting transfers between devices: 8.92 us -> none  [the longest x2 6.33 us: with_halo(): before = lax.ppermute(last, axis, up)]
    another operation x1 -> x0, loops' own time: 7.52 us -> none  [shade_slab(): lax.scan(advance, start, jnp.arange(count, dtype=jnp.int32))]
  transfers between devices with their start and end apart: 4 -> 0, of which waited for: 2 -> 0; matrix products, arithmetic and copies ran while one was open for 0% -> 0% of each run, Pallas kernels for 0% -> 0%
where the time goes in v1:
time: 116 us
  Pallas kernels  111 us (96%)
  local copies, waits for them, and re-layouts  4.85 us (4%)
    pallas_call x1, Pallas kernels, local(): pl.pallas_call(functools.partial(kernel, depth, rows), out_shape=jax.Shap...  111 us

profile of v1, /device:TPU:0, one launch (start us, length us, event | category | flops | bytes accessed | tf_op | source)
XLA Modules:
  0.0 115.5 jit_solution(6850811823681111677)
XLA Ops:
  0.0 1.3 %fusion = (f32[4,1,2048]{2,1,0:T(1,128)S(1)}, f32[4,1,2048]{2,1,0:T(1,128)S(1)}, f32[4,1,2048]{2,1,0:T(1,128)S(1)}, f32[4,1,2048]{2,1,0:T(1,128)S(1)}) fusion(f32[4,128,2048]{2,1,0:T(8,128)} %param.1), kind=kLoop, calls=%fused_computation.5 | loop fusion | bytes 262144 | tf_op jit(solution)/shard_map/slice | solution.py:378
  1.4 0.0 copy-start
  1.4 2.2 %copy-done = f32[4,128,2048]{2,1,0:T(8,128)S(1)} copy-done((f32[4,128,2048]{2,1,0:T(8,128)S(1)}, f32[4,128,2048]{2,1,0:T(8,128)}, u32[]{:S(2)}) %copy-start) | copy-done | bytes 4194328
  3.6 110.6 %shard_map.17 = f32[4,16,8,256]{3,2,1,0:T(8,128)S(1)} custom-call(f32[4,16,8,2048]{3,2,1,0:T(8,128)S(1)} %bitcast.10, f32[4,4,2048]{2,1,0:T(4,128)S(1)} %pad_maximum_fusion.edge_ref), custom_call_target="tpu_custom_call" | custom-call | tf_op jit(solution)/shard_map/pallas_call | solution.py:383
  114.2 1.3 %copy.6 = f32[4,128,1,256]{3,2,1,0:T(1,128)} copy(f32[4,128,1,256]{3,1,0,2:T(8,128)S(1)} %bitcast.11) | data formatting | bytes 1048576 | tf_op jit(solution)/shard_map/reshape | solution.py:407
  (3 shorter events, 0.1 us)
Async XLA Ops:
  1.4 2.2 %copy-start = (f32[4,128,2048]{2,1,0:T(8,128)S(1)}, f32[4,128,2048]{2,1,0:T(8,128)}, u32[]{:S(2)}) copy-start(f32[4,128,2048]{2,1,0:T(8,128)} %param.1) | copy-start | bytes 12582916

commit v2 on v1

--- a/solution.py
+++ b/solution.py
@@ -1,4 +1,5 @@
 import functools
+import math
 
 import jax
 import jax.numpy as jnp
@@ -11,6 +12,8 @@
 TILE = 8
 LANES = 128
 BLOCK = 256
+AHEAD = 3
+LOG2E = 1.4426950408889634
 
 
 def with_halo(shard, sides, width):
@@ -88,9 +91,10 @@
     chunks = tiles // 2
     groups = depth // 2
     steps = groups.bit_length() - 1
+    ahead = min(AHEAD, chunks)
     part = LANES * depth
     span = pl.ds(LANES, W)
-    extinction = 0.5 / (S * depth)
+    log_extinction = math.log2(0.5 / (S * depth) * LOG2E)
 
     held, came = rest[: steps + 1], rest[steps + 1 : 2 * steps + 1]
     (own_sem, own_edge_sem, pair_send, pair_recv, edge_send, edge_recv, row_send, row_recv,
@@ -188,7 +192,7 @@
 
     edge_copy().start()
 
-    @pl.loop(0, chunks)
+    @pl.loop(0, ahead)
     def _(c):
         pair_copy(c).start()
 
@@ -250,7 +254,7 @@
         def columns(b, carry):
             base = pl.multiple_of(b * BLOCK, BLOCK)
             mid = pl.ds(pl.multiple_of(base + LANES, LANES), BLOCK)
-            red = green = blue = alpha = jnp.zeros((TILE, BLOCK), jnp.float32)
+            both = swing = green = alpha = jnp.zeros((TILE, BLOCK), jnp.float32)
             before = cells[0, t, :, mid]
             wide = cells[1, t, :, pl.ds(base, BLOCK + 2 * LANES)]
             for s in range(1, 2 * S + 1):
@@ -265,20 +269,19 @@
                 above = jnp.where(is_top, cells[s, t - 1, TILE - 1 : TILE, mid], pltpu.roll(centre, 1, 0))
                 below = jnp.where(is_bottom, cells[s, t + 1, 0:1, mid], pltpu.roll(centre, TILE - 1, 0))
                 dz, dy, dx = after - before, below - above, right - left
-                square = dz * dz + dy * dy + dx * dx + 4.0
-                facing = 0.42 * dz + 0.336 * dy + 0.448 * dx
-                shading = 0.3 + jnp.abs(facing) * lax.rsqrt(square)
-                opacity = 1.0 - jnp.exp(-extinction * jnp.exp(1.5 * centre))
+                square = dz * dz + dy * dy + (dx * dx + 4.0)
+                facing = 1.25 * dz + dy + (0.64 / 0.48) * dx
+                shading = jnp.abs(facing) * lax.rsqrt(square) + 0.3 / 0.336
+                opacity = 1.0 - jnp.exp2(-jnp.exp2((1.5 * LOG2E) * centre + log_extinction))
                 weight = (1.0 - alpha) * opacity
                 lit = weight * shading
-                half = 0.5 * lit
-                swing = half * jnp.tanh(centre)
-                red = red + (half + swing)
-                green = green + lit * jnp.exp(-centre * centre)
-                blue = blue + (half - swing)
+                both = both + lit
+                swing = swing + lit * jnp.tanh(centre)
+                green = green + lit * jnp.exp2(centre * (centre * -LOG2E))
                 alpha = alpha + weight
                 before, wide = centre, wide_after
-            for ch, value in enumerate((red, green, blue, alpha)):
+            both, swing = (0.5 * 0.336) * both, (0.5 * 0.336) * swing
+            for ch, value in enumerate((both + swing, 0.336 * green, both - swing, alpha)):
                 image[ch, :, pl.ds(base, BLOCK)] = value
             return carry
 
@@ -325,6 +328,7 @@
         @pl.when(i < chunks)
         def _():
             pair_copy(i).wait_recv()
+            pl.when(i + ahead < chunks)(lambda: pair_copy(i + ahead).start())
             pl.when(has_next)(lambda: face_copy(0, i).start())
             pl.when(has_prev)(lambda: face_copy(1, i).start())
 
@@ -401,7 +405,7 @@
             DMA((chunks,)), DMA((chunks,)),
         ],
         compiler_params=pltpu.CompilerParams(
-            collective_id=0, has_side_effects=True, vmem_limit_bytes=40 * 1024 * 1024
+            collective_id=0, has_side_effects=True, vmem_limit_bytes=60 * 1024 * 1024
         ),
     )(log_density.reshape(S, tiles, TILE, W), edge_rows)
     return out.reshape(4, R, 1, Cw)

time: 116 us -> 88 us (0.76)
  Pallas kernels: 111 us -> 83.4 us
    pallas_call x1, Pallas kernels: 111 us -> 83.4 us  [local(): pl.pallas_call(functools.partial(kernel, depth, rows), out_shape=jax.Shap...]
    unnamed x2 -> x0, local copies, waits for them, and re-layouts: 2.18 us -> none
where the time goes in v2:
time: 88 us; the launch traced here: 87.8 us
  Pallas kernels  83.4 us (95%)
  local copies, waits for them, and re-layouts  3.71 us (4%)
    pallas_call x1, Pallas kernels, local(): pl.pallas_call(functools.partial(kernel, depth, rows), out_shape=jax.Shap...  83.4 us
    reshape x1, local copies, waits for them, and re-layouts, local(): return out.reshape(4, R, 1, Cw)  2.37 us

profile of v2, /device:TPU:0, one launch (start us, length us, event | category | flops | bytes accessed | tf_op | source)
XLA Modules:
  0.0 87.8 jit_solution(14226700465209791767)
XLA Ops:
  0.0 1.3 %fusion = (f32[4,1,2048]{2,1,0:T(1,128)S(1)}, f32[4,1,2048]{2,1,0:T(1,128)S(1)}, f32[4,1,2048]{2,1,0:T(1,128)S(1)}, f32[4,1,2048]{2,1,0:T(1,128)S(1)}) fusion(f32[4,128,2048]{2,1,0:T(8,128)} %param.1), kind=kLoop, calls=%fused_computation.5 | loop fusion | bytes 262144 | tf_op jit(solution)/shard_map/slice | solution.py:382
  1.4 0.7 pad_maximum_fusion.edge_ref
  2.0 83.4 %shard_map.17 = f32[4,16,8,256]{3,2,1,0:T(8,128)} custom-call(f32[4,16,8,2048]{3,2,1,0:T(8,128)} %bitcast.10, f32[4,4,2048]{2,1,0:T(4,128)} %pad_maximum_fusion.edge_ref), custom_call_target="tpu_custom_call" | custom-call | tf_op jit(solution)/shard_map/pallas_call | solution.py:387
  85.5 2.4 %copy.6 = f32[4,128,1,256]{3,2,1,0:T(1,128)} copy(f32[4,128,1,256]{3,1,0,2:T(8,128)} %bitcast.11) | data formatting | bytes 1048576 | tf_op jit(solution)/shard_map/reshape | solution.py:411
  (2 shorter events, 0.1 us)

commit v3 on v2

--- a/solution.py
+++ b/solution.py
@@ -86,18 +86,20 @@
     return sum(((value >> b) & 1) << (bits - 1 - b) for b in range(bits))
 
 
-def kernel(depth, rows, vol_ref, edge_ref, out_ref, cells, edges, spread, image, *rest):
+def kernel(depth, rows, vol_ref, out_ref, cells, edges, rim, cut, spread, image, final, *rest):
     S, tiles, _, W = vol_ref.shape
     chunks = tiles // 2
     groups = depth // 2
     steps = groups.bit_length() - 1
-    ahead = min(AHEAD, chunks)
     part = LANES * depth
+    parts = W // part
+    pieces = parts * chunks
+    ahead = min(AHEAD, pieces)
     span = pl.ds(LANES, W)
     log_extinction = math.log2(0.5 / (S * depth) * LOG2E)
 
     held, came = rest[: steps + 1], rest[steps + 1 : 2 * steps + 1]
-    (own_sem, own_edge_sem, pair_send, pair_recv, edge_send, edge_recv, row_send, row_recv,
+    (own_sem, rim_sem, own_edge_sem, pair_send, pair_recv, edge_send, edge_recv, row_send, row_recv,
      face_send, face_recv, part_send, part_recv, last_send, last_recv) = rest[2 * steps + 1 :]
 
     me, row = lax.axis_index("depth"), lax.axis_index("rows")
@@ -107,8 +109,7 @@
     mine = 1 + S * x
 
     near = [(partner, row, None)]
-    offsets = [(-1, z >= 1), (1, z <= groups - 2)]
-    for d, there in offsets:
+    for d, there in ((-1, z >= 1), (1, z <= groups - 2)):
         near.append((me + 2 * d, row, there))
     for k in range(1, steps):
         near.append((2 * (z + (1 << k) * (1 - 2 * (lax.rem(z // (1 << k), 2)))) + x, row, None))
@@ -133,74 +134,99 @@
         own_sem,
     )
     own.start()
-    own_edge = pltpu.make_async_copy(edge_ref.at[2 - x], edges.at[1 - x, x], own_edge_sem)
-    own_edge.start()
+    rims = [
+        pltpu.make_async_copy(vol_ref.at[:, tile], rim.at[n], rim_sem.at[n])
+        for n, tile in enumerate(((1 - x) * chunks, (2 - x) * chunks - 1))
+    ]
+    for copy in rims:
+        copy.start()
     pl.semaphore_wait(barrier, count)
 
-    def pair_copy(c):
-        return pltpu.make_async_remote_copy(
-            src_ref=vol_ref.at[:, (1 - x) * chunks + c],
-            dst_ref=cells.at[pl.ds(mine, S), 1 + c, :, span],
-            send_sem=pair_send.at[c], recv_sem=pair_recv.at[c],
-            device_id=(partner, row), device_id_type=MESH,
-        )
+    def pair_copy(q):
+        def apply(act):
+            for g in range(parts):
+                low = g * part + (LANES if g else 0)
+                high = (g + 1) * part + (LANES if g + 1 < parts else 0)
+
+                @pl.when(q // chunks == g)
+                def _(g=g, low=low, high=high):
+                    c = q - g * chunks
+                    act(pltpu.make_async_remote_copy(
+                        src_ref=vol_ref.at[:, (1 - x) * chunks + c, :, pl.ds(low, high - low)],
+                        dst_ref=cells.at[pl.ds(mine, S), 1 + c, :, pl.ds(LANES + low, high - low)],
+                        send_sem=pair_send.at[q], recv_sem=pair_recv.at[q],
+                        device_id=(partner, row), device_id_type=MESH,
+                    ))
+        return apply
+
+    def start(copy):
+        copy.start()
 
     def edge_copy():
         return pltpu.make_async_remote_copy(
-            src_ref=edge_ref.at[1 + x], dst_ref=edges.at[x, x],
+            src_ref=cut.at[1 + x], dst_ref=edges.at[x, x],
             send_sem=edge_send, recv_sem=edge_recv,
             device_id=(partner, row), device_id_type=MESH,
         )
 
     def row_copy(direction):
         return pltpu.make_async_remote_copy(
-            src_ref=edge_ref.at[3 - 3 * direction], dst_ref=edges.at[direction, x],
+            src_ref=cut.at[3 - 3 * direction], dst_ref=edges.at[direction, x],
             send_sem=row_send.at[direction], recv_sem=row_recv.at[x],
             device_id=(first + direction, row + 1 - 2 * direction), device_id_type=MESH,
         )
 
     def row_arrival(source):
         return pltpu.make_async_remote_copy(
-            src_ref=edge_ref.at[0], dst_ref=edges.at[x, source],
+            src_ref=cut.at[0], dst_ref=edges.at[x, source],
             send_sem=row_send.at[0], recv_sem=row_recv.at[source],
             device_id=(partner, row), device_id_type=MESH,
         )
 
-    def face_copy(direction, c):
-        return pltpu.make_async_remote_copy(
-            src_ref=cells.at[2 * S if direction == 0 else 1, 1 + c, :, span],
-            dst_ref=cells.at[0 if direction == 0 else 2 * S + 1, 1 + c, :, span],
-            send_sem=face_send.at[direction, c], recv_sem=face_recv.at[direction, c],
+    def face_copy(direction, q):
+        c, at = lax.rem(q, chunks), pl.ds(pl.multiple_of(LANES + q // chunks * part, LANES), part)
+        return pltpu.make_async_remote_copy(
+            src_ref=cells.at[2 * S if direction == 0 else 1, 1 + c, :, at],
+            dst_ref=cells.at[0 if direction == 0 else 2 * S + 1, 1 + c, :, at],
+            send_sem=face_send.at[direction, q], recv_sem=face_recv.at[direction, q],
             device_id=(me + (2 if direction == 0 else -2), row), device_id_type=MESH,
         )
 
-    def part_copy(k, c):
+    def part_copy(k, q):
         half = groups >> (k + 1)
         bit = lax.rem(z // (1 << k), 2)
         return pltpu.make_async_remote_copy(
-            src_ref=held[k].at[c, pl.ds((1 - bit) * half, half)], dst_ref=came[k].at[c],
-            send_sem=part_send.at[k, c], recv_sem=part_recv.at[k, c],
+            src_ref=held[k].at[q, pl.ds((1 - bit) * half, half)], dst_ref=came[k].at[q],
+            send_sem=part_send.at[k, q], recv_sem=part_recv.at[k, q],
             device_id=(me + 2 * (1 << k) * (1 - 2 * bit), row), device_id_type=MESH,
         )
 
-    def last_copy(c):
-        return pltpu.make_async_remote_copy(
-            src_ref=held[steps].at[c, 0, 1 - x], dst_ref=out_ref.at[:, x * chunks + c],
-            send_sem=last_send.at[c], recv_sem=last_recv.at[c],
+    def last_copy(q):
+        return pltpu.make_async_remote_copy(
+            src_ref=held[steps].at[q, 0, 1 - x], dst_ref=final.at[q],
+            send_sem=last_send.at[q], recv_sem=last_recv.at[q],
             device_id=(partner, row), device_id_type=MESH,
         )
 
-    edge_copy().start()
-
-    @pl.loop(0, ahead)
-    def _(c):
-        pair_copy(c).start()
+    pl.loop(0, ahead)(lambda q: pair_copy(q)(start))
 
     has_next_row, has_prev_row = row <= rows - 2, row >= 1
     has_next, has_prev = z <= groups - 2, z >= 1
     has_edge = jnp.logical_or(jnp.logical_and(x == 0, has_prev_row), jnp.logical_and(x == 1, has_next_row))
+
+    own.wait()
+    for copy in rims:
+        copy.wait()
+    for s in range(S):
+        cut[2 * x, s : s + 1, :] = cells[mine + s, 1, 0:1, LANES : LANES + W]
+        cut[1 + 2 * x, s : s + 1, :] = cells[mine + s, chunks, TILE - 1 : TILE, LANES : LANES + W]
+        cut[2 - 2 * x, s : s + 1, :] = rim[0, s, 0:1, :]
+        cut[3 - 2 * x, s : s + 1, :] = rim[1, s, TILE - 1 : TILE, :]
+    edge_copy().start()
     pl.when(has_next_row)(lambda: row_copy(0).start())
     pl.when(has_prev_row)(lambda: row_copy(1).start())
+    own_edge = pltpu.make_async_copy(cut.at[2 - x], edges.at[1 - x, x], own_edge_sem)
+    own_edge.start()
 
     @pl.loop(0, 2 * S + 2)
     def _(s):
@@ -226,7 +252,6 @@
         source = (to % LANES) * depth + to // LANES
         spread[pl.ds(pl.multiple_of(b * 16, 16), 16), :] = jnp.where(at == source, 1.0, 0.0).astype(jnp.bfloat16)
 
-    own.wait()
     own_edge.wait()
     edge_copy().wait()
     pl.when(has_next_row)(lambda: row_copy(0).wait_send())
@@ -248,11 +273,11 @@
     row_of = lax.broadcasted_iota(jnp.int32, (TILE, BLOCK), 0)
     is_top, is_bottom = row_of == 0, row_of == TILE - 1
 
-    def shade(c):
-        t = 1 + c
+    def shade(q):
+        t, begin = 1 + lax.rem(q, chunks), q // chunks * part
 
         def columns(b, carry):
-            base = pl.multiple_of(b * BLOCK, BLOCK)
+            base = pl.multiple_of(begin + b * BLOCK, BLOCK)
             mid = pl.ds(pl.multiple_of(base + LANES, LANES), BLOCK)
             both = swing = green = alpha = jnp.zeros((TILE, BLOCK), jnp.float32)
             before = cells[0, t, :, mid]
@@ -282,29 +307,24 @@
                 before, wide = centre, wide_after
             both, swing = (0.5 * 0.336) * both, (0.5 * 0.336) * swing
             for ch, value in enumerate((both + swing, 0.336 * green, both - swing, alpha)):
-                image[ch, :, pl.ds(base, BLOCK)] = value
+                image[ch, :, pl.ds(pl.multiple_of(b * BLOCK, BLOCK), BLOCK)] = value
             return carry
 
-        lax.fori_loop(0, W // BLOCK, columns, 0)
-        for g in range(W // part):
-            piece = image[:, :, g * part : (g + 1) * part].reshape(4 * TILE, part)
-            high = piece.astype(jnp.bfloat16)
-            low = (piece - high.astype(jnp.float32)).astype(jnp.bfloat16)
-            both = jnp.dot(
-                jnp.concatenate([high, low], axis=0), spread[...], preferred_element_type=jnp.float32
-            )
-            sorted_ = both[: 4 * TILE] + both[4 * TILE :]
-            for j in range(depth):
-                place = bit_reversed(j // 2, steps)
-                held[0][c, place, j % 2, :, :, g * LANES : (g + 1) * LANES] = sorted_[
-                    :, j * LANES : (j + 1) * LANES
-                ].reshape(4, TILE, LANES)
-
-    def combine(k, c):
+        lax.fori_loop(0, part // BLOCK, columns, 0)
+        piece = image[...].reshape(4 * TILE, part)
+        high = piece.astype(jnp.bfloat16)
+        low = (piece - high.astype(jnp.float32)).astype(jnp.bfloat16)
+        two = jnp.dot(jnp.concatenate([high, low], axis=0), spread[...], preferred_element_type=jnp.float32)
+        by_class = two[: 4 * TILE] + two[4 * TILE :]
+        for j in range(depth):
+            held[0][q, bit_reversed(j // 2, steps), j % 2] = by_class[
+                :, j * LANES : (j + 1) * LANES
+            ].reshape(4, TILE, LANES)
+
+    def combine(k, q):
         half = groups >> (k + 1)
         bit = lax.rem(z // (1 << k), 2)
-        copy = part_copy(k, c)
-        copy.wait_recv()
+        part_copy(k, q).wait_recv()
 
         def join(near_of, far_of):
             for i in range(half):
@@ -312,54 +332,60 @@
                     near, far = near_of(i, p), far_of(i, p)
                     clear = 1.0 - near[3]
                     for ch in range(4):
-                        held[k + 1][c, i, p, ch] = near[ch] + clear * far[ch]
+                        held[k + 1][q, i, p, ch] = near[ch] + clear * far[ch]
 
         def kept(i, p):
-            return held[k][c, bit * half + i, p]
+            return held[k][q, bit * half + i, p]
 
         def received(i, p):
-            return came[k][c, i, p]
+            return came[k][q, i, p]
 
         pl.when(bit == 0)(lambda: join(kept, received))
         pl.when(bit == 1)(lambda: join(received, kept))
 
-    @pl.loop(0, chunks + steps + 1)
+    def put(side, q, value):
+        at = ((side * chunks + lax.rem(q, chunks)) * TILE) * parts + q // chunks
+        for ch in range(4):
+            out_ref[ch, pl.ds(at, TILE, stride=parts), :] = value[ch]
+
+    @pl.loop(0, pieces + steps + 1)
     def _(i):
-        @pl.when(i < chunks)
+        @pl.when(i < pieces)
         def _():
-            pair_copy(i).wait_recv()
-            pl.when(i + ahead < chunks)(lambda: pair_copy(i + ahead).start())
+            pair_copy(i)(lambda copy: copy.wait_recv())
+            pl.when(i + ahead < pieces)(lambda: pair_copy(i + ahead)(start))
             pl.when(has_next)(lambda: face_copy(0, i).start())
             pl.when(has_prev)(lambda: face_copy(1, i).start())
 
-        @pl.when(jnp.logical_and(i >= 1, i <= chunks))
+        @pl.when(jnp.logical_and(i >= 1, i <= pieces))
         def _():
-            c = i - 1
-            pl.when(has_prev)(lambda: face_copy(0, c).wait_recv())
-            pl.when(has_next)(lambda: face_copy(1, c).wait_recv())
-            shade(c)
-            part_copy(0, c).start()
+            q = i - 1
+            pl.when(has_prev)(lambda: face_copy(0, q).wait_recv())
+            pl.when(has_next)(lambda: face_copy(1, q).wait_recv())
+            shade(q)
+            part_copy(0, q).start()
 
         for k in range(steps):
 
-            @pl.when(jnp.logical_and(i >= k + 2, i <= chunks + k + 1))
+            @pl.when(jnp.logical_and(i >= k + 2, i <= pieces + k + 1))
             def _(k=k):
-                c = i - 2 - k
-                combine(k, c)
+                q = i - 2 - k
+                combine(k, q)
                 if k + 1 < steps:
-                    part_copy(k + 1, c).start()
+                    part_copy(k + 1, q).start()
                 else:
-                    out_ref[:, x * chunks + c] = held[steps][c, 0, x]
-                    last_copy(c).start()
-
-    @pl.loop(0, chunks)
-    def _(c):
-        pair_copy(c).wait_send()
-        pl.when(has_next)(lambda: face_copy(0, c).wait_send())
-        pl.when(has_prev)(lambda: face_copy(1, c).wait_send())
+                    last_copy(q).start()
+                    put(x, q, held[steps][q, 0, x])
+
+    @pl.loop(0, pieces)
+    def _(q):
+        pair_copy(q)(lambda copy: copy.wait_send())
+        pl.when(has_next)(lambda: face_copy(0, q).wait_send())
+        pl.when(has_prev)(lambda: face_copy(1, q).wait_send())
         for k in range(steps):
-            part_copy(k, c).wait_send()
-        last_copy(c).wait()
+            part_copy(k, q).wait_send()
+        last_copy(q).wait()
+        put(1 - x, q, final[q])
 
 
 def local(log_density):
@@ -370,7 +396,6 @@
         depth >= 4
         and depth & (depth - 1) == 0
         and W % (LANES * depth) == 0
-        and W % BLOCK == 0
         and R % (2 * TILE) == 0
     )
     if not fits:
@@ -378,37 +403,41 @@
     steps = groups.bit_length() - 1
     tiles = R // TILE
     chunks = tiles // 2
-    Cw = W // depth
-    edge_rows = jnp.stack([log_density[:, r] for r in (0, R // 2 - 1, R // 2, R - 1)])
+    part = LANES * depth
+    parts = W // part
+    pieces = parts * chunks
     F32 = jnp.float32
-    parts = [pltpu.VMEM((chunks, groups >> k, 2, 4, TILE, Cw), F32) for k in range(steps + 1)]
-    arrivals = [pltpu.VMEM((chunks, groups >> (k + 1), 2, 4, TILE, Cw), F32) for k in range(steps)]
+    partial = [pltpu.VMEM((pieces, groups >> k, 2, 4, TILE, LANES), F32) for k in range(steps + 1)]
+    arrivals = [pltpu.VMEM((pieces, groups >> (k + 1), 2, 4, TILE, LANES), F32) for k in range(steps)]
     DMA = pltpu.SemaphoreType.DMA
     out = pl.pallas_call(
         functools.partial(kernel, depth, rows),
-        out_shape=jax.ShapeDtypeStruct((4, tiles, TILE, Cw), F32),
-        in_specs=[pl.BlockSpec(memory_space=pl.ANY)] * 2,
+        out_shape=jax.ShapeDtypeStruct((4, R * parts, LANES), F32),
+        in_specs=[pl.BlockSpec(memory_space=pl.ANY)],
         out_specs=pl.BlockSpec(memory_space=pltpu.VMEM),
         scratch_shapes=[
             pltpu.VMEM((2 * S + 2, chunks + 2, TILE, W + 2 * LANES), F32),
             pltpu.VMEM((2, 2, S, W), F32),
-            pltpu.VMEM((LANES * depth, LANES * depth), jnp.bfloat16),
-            pltpu.VMEM((4, TILE, W), F32),
-            *parts,
+            pltpu.VMEM((2, S, TILE, W), F32),
+            pltpu.VMEM((4, S, W), F32),
+            pltpu.VMEM((part, part), jnp.bfloat16),
+            pltpu.VMEM((4, TILE, part), F32),
+            pltpu.VMEM((pieces, 4, TILE, LANES), F32),
+            *partial,
             *arrivals,
-            DMA, DMA,
-            DMA((chunks,)), DMA((chunks,)),
+            DMA, DMA((2,)), DMA,
+            DMA((pieces,)), DMA((pieces,)),
             DMA, DMA,
             DMA((2,)), DMA((2,)),
-            DMA((2, chunks)), DMA((2, chunks)),
-            DMA((steps, chunks)), DMA((steps, chunks)),
-            DMA((chunks,)), DMA((chunks,)),
+            DMA((2, pieces)), DMA((2, pieces)),
+            DMA((steps, pieces)), DMA((steps, pieces)),
+            DMA((pieces,)), DMA((pieces,)),
         ],
         compiler_params=pltpu.CompilerParams(
             collective_id=0, has_side_effects=True, vmem_limit_bytes=60 * 1024 * 1024
         ),
-    )(log_density.reshape(S, tiles, TILE, W), edge_rows)
-    return out.reshape(4, R, 1, Cw)
+    )(log_density.reshape(S, tiles, TILE, W))
+    return out.reshape(4, R, 1, W // depth)
 
 
 def solution(mesh):

time: 88 us -> 82.8 us (0.941)
  Pallas kernels: 83.4 us -> 80.4 us
  local copies, waits for them, and re-layouts: 3.71 us -> 2.19 us
    pallas_call x1, Pallas kernels: 83.4 us -> 80.4 us  [local(): pl.pallas_call(functools.partial(kernel, depth, rows), out_shape=jax.Shap...]
    reshape x1 -> x0, local copies, waits for them, and re-layouts: 2.37 us -> none  [local(): return out.reshape(4, R, 1, Cw)]
    unnamed x0 -> x1, local copies, waits for them, and re-layouts: none -> 2.19 us
    slice x1 -> x0, local copies, waits for them, and re-layouts: 1.28 us -> none  [local(): log_density[:, r]]
where the time goes in v3:
time: 82.8 us; the launch traced here: 82.6 us
  Pallas kernels  80.4 us (97%)
  local copies, waits for them, and re-layouts  2.19 us (3%)
    pallas_call x1, Pallas kernels, local(): pl.pallas_call(functools.partial(kernel, depth, rows), out_shape=jax.Shap...  80.4 us
    unnamed x1, local copies, waits for them, and re-layouts  2.19 us

profile of v3, /device:TPU:0, one launch (start us, length us, event | category | flops | bytes accessed | tf_op | source)
XLA Modules:
  0.0 82.6 jit_solution(13606922060420712763)
XLA Ops:
  0.0 80.4 %shard_map.17 = f32[4,256,128]{2,1,0:T(8,128)} custom-call(f32[4,16,8,2048]{3,2,1,0:T(8,128)} %bitcast.2), custom_call_target="tpu_custom_call" | custom-call | tf_op jit(solution)/shard_map/pallas_call | solution.py:413
  80.4 2.2 %copy.4 = f32[4,128,1,256]{3,2,1,0:T(1,128)} copy(f32[4,128,1,256]{3,2,1,0:T(1,128)} %bitcast.3) | data formatting | bytes 1048576

commit v4 on v3

--- a/solution.py
+++ b/solution.py
@@ -12,7 +12,7 @@
 TILE = 8
 LANES = 128
 BLOCK = 256
-AHEAD = 3
+AHEAD = 6
 LOG2E = 1.4426950408889634
 
 

time: 82.8 us -> 92.3 us (1.11)
  Pallas kernels: 80.4 us -> 89.9 us
    pallas_call x1, Pallas kernels: 80.4 us -> 89.9 us  [local(): pl.pallas_call(functools.partial(kernel, depth, rows), out_shape=jax.Shap...]
where the time goes in v4:
time: 92.3 us; the launch traced here: 92.1 us
  Pallas kernels  89.9 us (97%)
  local copies, waits for them, and re-layouts  2.19 us (2%)
    pallas_call x1, Pallas kernels, local(): pl.pallas_call(functools.partial(kernel, depth, rows), out_shape=jax.Shap...  89.9 us
    unnamed x1, local copies, waits for them, and re-layouts  2.19 us

profile of v4, /device:TPU:0, one launch (start us, length us, event | category | flops | bytes accessed | tf_op | source)
XLA Modules:
  0.0 92.1 jit_solution(11402028732094229235)
XLA Ops:
  0.0 89.9 %shard_map.17 = f32[4,256,128]{2,1,0:T(8,128)} custom-call(f32[4,16,8,2048]{3,2,1,0:T(8,128)} %bitcast.2), custom_call_target="tpu_custom_call" | custom-call | tf_op jit(solution)/shard_map/pallas_call | solution.py:413
  89.9 2.2 %copy.4 = f32[4,128,1,256]{3,2,1,0:T(1,128)} copy(f32[4,128,1,256]{3,2,1,0:T(1,128)} %bitcast.3) | data formatting | bytes 1048576

commit v5 on v4

--- a/solution.py
+++ b/solution.py
@@ -12,7 +12,7 @@
 TILE = 8
 LANES = 128
 BLOCK = 256
-AHEAD = 6
+AHEAD = 2
 LOG2E = 1.4426950408889634
 
 
@@ -245,12 +245,15 @@
         def _(c):
             cells[2 * S + 1, 1 + c, :, span] = jnp.zeros((TILE, W), jnp.float32)
 
-    @pl.loop(0, part // 16)
+    blocks, group = part // BLOCK, BLOCK // depth
+
+    @pl.loop(0, blocks)
     def _(b):
-        at = lax.broadcasted_iota(jnp.int32, (16, part), 0) + b * 16
-        to = lax.broadcasted_iota(jnp.int32, (16, part), 1)
-        source = (to % LANES) * depth + to // LANES
-        spread[pl.ds(pl.multiple_of(b * 16, 16), 16), :] = jnp.where(at == source, 1.0, 0.0).astype(jnp.bfloat16)
+        at = lax.broadcasted_iota(jnp.int32, (BLOCK, BLOCK), 0)
+        to = lax.broadcasted_iota(jnp.int32, (BLOCK, BLOCK), 1)
+        klass = to // LANES * blocks + (to % LANES // group + blocks - b) % blocks
+        source = to % group * depth + klass
+        spread[b] = jnp.where(at == source, 1.0, 0.0).astype(jnp.bfloat16)
 
     own_edge.wait()
     edge_copy().wait()
@@ -270,56 +273,75 @@
         cells[1 + s, 0, TILE - 1 : TILE, LANES : LANES + W] = edges[0, s // S, s % S : s % S + 1, :]
         cells[1 + s, chunks + 1, 0:1, LANES : LANES + W] = edges[1, s // S, s % S : s % S + 1, :]
 
-    row_of = lax.broadcasted_iota(jnp.int32, (TILE, BLOCK), 0)
+    row_of = lax.broadcasted_iota(jnp.int32, (TILE, LANES), 0)
+    lane_of = lax.broadcasted_iota(jnp.int32, (TILE, LANES), 1)
     is_top, is_bottom = row_of == 0, row_of == TILE - 1
+    is_left, is_right = lane_of == 0, lane_of == LANES - 1
+    group_of = lax.broadcasted_iota(jnp.int32, (4 * TILE, LANES), 1) // group
 
     def shade(q):
         t, begin = 1 + lax.rem(q, chunks), q // chunks * part
 
         def columns(b, carry):
             base = pl.multiple_of(begin + b * BLOCK, BLOCK)
-            mid = pl.ds(pl.multiple_of(base + LANES, LANES), BLOCK)
-            both = swing = green = alpha = jnp.zeros((TILE, BLOCK), jnp.float32)
-            before = cells[0, t, :, mid]
-            wide = cells[1, t, :, pl.ds(base, BLOCK + 2 * LANES)]
+
+            def lanes(v):
+                return pl.ds(pl.multiple_of(base + v * LANES, LANES), LANES)
+
+            def load(s):
+                return [cells[s, t, :, lanes(v)] for v in range(BLOCK // LANES + 2)]
+
+            zero = jnp.zeros((TILE, LANES), jnp.float32)
+            sums = [[zero] * 4 for _ in range(BLOCK // LANES)]
+            before, here = load(0), load(1)
             for s in range(1, 2 * S + 1):
-                centre = wide[:, LANES : LANES + BLOCK]
-                if s < 2 * S:
-                    wide_after = cells[s + 1, t, :, pl.ds(base, BLOCK + 2 * LANES)]
-                    after = wide_after[:, LANES : LANES + BLOCK]
-                else:
-                    wide_after, after = None, cells[s + 1, t, :, mid]
-                left = pltpu.roll(wide, 1, 1)[:, LANES : LANES + BLOCK]
-                right = pltpu.roll(wide, BLOCK + 2 * LANES - 1, 1)[:, LANES : LANES + BLOCK]
-                above = jnp.where(is_top, cells[s, t - 1, TILE - 1 : TILE, mid], pltpu.roll(centre, 1, 0))
-                below = jnp.where(is_bottom, cells[s, t + 1, 0:1, mid], pltpu.roll(centre, TILE - 1, 0))
-                dz, dy, dx = after - before, below - above, right - left
-                square = dz * dz + dy * dy + (dx * dx + 4.0)
-                facing = 1.25 * dz + dy + (0.64 / 0.48) * dx
-                shading = jnp.abs(facing) * lax.rsqrt(square) + 0.3 / 0.336
-                opacity = 1.0 - jnp.exp2(-jnp.exp2((1.5 * LOG2E) * centre + log_extinction))
-                weight = (1.0 - alpha) * opacity
-                lit = weight * shading
-                both = both + lit
-                swing = swing + lit * jnp.tanh(centre)
-                green = green + lit * jnp.exp2(centre * (centre * -LOG2E))
-                alpha = alpha + weight
-                before, wide = centre, wide_after
-            both, swing = (0.5 * 0.336) * both, (0.5 * 0.336) * swing
-            for ch, value in enumerate((both + swing, 0.336 * green, both - swing, alpha)):
-                image[ch, :, pl.ds(pl.multiple_of(b * BLOCK, BLOCK), BLOCK)] = value
+                after = load(s + 1)
+                for v in range(BLOCK // LANES):
+                    both, swing, green, alpha = sums[v]
+                    centre = here[v + 1]
+                    left = pltpu.roll(jnp.where(is_right, here[v], centre), 1, 1)
+                    right = pltpu.roll(jnp.where(is_left, here[v + 2], centre), LANES - 1, 1)
+                    above = pltpu.roll(jnp.where(is_bottom, cells[s, t - 1, :, lanes(v + 1)], centre), 1, 0)
+                    below = pltpu.roll(jnp.where(is_top, cells[s, t + 1, :, lanes(v + 1)], centre), TILE - 1, 0)
+                    dz, dy, dx = after[v + 1] - before[v + 1], below - above, right - left
+                    square = dz * dz + dy * dy + (dx * dx + 4.0)
+                    facing = 1.25 * dz + dy + (0.64 / 0.48) * dx
+                    shading = jnp.abs(facing) * lax.rsqrt(square) + 0.3 / 0.336
+                    opacity = 1.0 - jnp.exp2(-jnp.exp2((1.5 * LOG2E) * centre + log_extinction))
+                    weight = (1.0 - alpha) * opacity
+                    lit = weight * shading
+                    sums[v] = [
+                        both + lit,
+                        swing + lit * jnp.tanh(centre),
+                        green + lit * jnp.exp2(centre * (centre * -LOG2E)),
+                        alpha + weight,
+                    ]
+                before, here = here, after
+            for v in range(BLOCK // LANES):
+                both, swing, green, alpha = sums[v]
+                both, swing = (0.5 * 0.336) * both, (0.5 * 0.336) * swing
+                to = pl.ds(pl.multiple_of(b * BLOCK + v * LANES, LANES), LANES)
+                for ch, value in enumerate((both + swing, 0.336 * green, both - swing, alpha)):
+                    image[ch, :, to] = value
             return carry
 
-        lax.fori_loop(0, part // BLOCK, columns, 0)
-        piece = image[...].reshape(4 * TILE, part)
-        high = piece.astype(jnp.bfloat16)
-        low = (piece - high.astype(jnp.float32)).astype(jnp.bfloat16)
-        two = jnp.dot(jnp.concatenate([high, low], axis=0), spread[...], preferred_element_type=jnp.float32)
-        by_class = two[: 4 * TILE] + two[4 * TILE :]
+        lax.fori_loop(0, blocks, columns, 0)
+        turned = []
+        for b in range(blocks):
+            piece = image[:, :, b * BLOCK : (b + 1) * BLOCK].reshape(4 * TILE, BLOCK)
+            high = piece.astype(jnp.bfloat16)
+            low = (piece - high.astype(jnp.float32)).astype(jnp.bfloat16)
+            two = jnp.dot(jnp.concatenate([high, low], axis=0), spread[b], preferred_element_type=jnp.float32)
+            turned.append(two[: 4 * TILE] + two[4 * TILE :])
         for j in range(depth):
-            held[0][q, bit_reversed(j // 2, steps), j % 2] = by_class[
-                :, j * LANES : (j + 1) * LANES
-            ].reshape(4, TILE, LANES)
+            h, r = j // blocks, j % blocks
+            mixed = turned[-r % blocks][:, h * LANES : (h + 1) * LANES]
+            for g in range(1, blocks):
+                other = turned[(g - r) % blocks][:, h * LANES : (h + 1) * LANES]
+                mixed = jnp.where(group_of == g, other, mixed)
+            if r:
+                mixed = pltpu.roll(mixed, LANES - group * r, 1)
+            held[0][q, bit_reversed(j // 2, steps), j % 2] = mixed.reshape(4, TILE, LANES)
 
     def combine(k, q):
         half = groups >> (k + 1)
@@ -393,7 +415,7 @@
     depth, rows = lax.axis_size("depth"), lax.axis_size("rows")
     groups = depth // 2
     fits = (
-        depth >= 4
+        4 <= depth <= LANES
         and depth & (depth - 1) == 0
         and W % (LANES * depth) == 0
         and R % (2 * TILE) == 0
@@ -420,7 +442,7 @@
             pltpu.VMEM((2, 2, S, W), F32),
             pltpu.VMEM((2, S, TILE, W), F32),
             pltpu.VMEM((4, S, W), F32),
-            pltpu.VMEM((part, part), jnp.bfloat16),
+            pltpu.VMEM((part // BLOCK, BLOCK, BLOCK), jnp.bfloat16),
             pltpu.VMEM((4, TILE, part), F32),
             pltpu.VMEM((pieces, 4, TILE, LANES), F32),
             *partial,
@@ -434,7 +456,7 @@
             DMA((pieces,)), DMA((pieces,)),
         ],
         compiler_params=pltpu.CompilerParams(
-            collective_id=0, has_side_effects=True, vmem_limit_bytes=60 * 1024 * 1024
+            collective_id=0, has_side_effects=True, vmem_limit_bytes=52 * 1024 * 1024
         ),
     )(log_density.reshape(S, tiles, TILE, W))
     return out.reshape(4, R, 1, W // depth)

time: 92.3 us -> 76.3 us (0.83)
  Pallas kernels: 89.9 us -> 75.3 us
  local copies, waits for them, and re-layouts: 2.19 us -> 0.8 us
    pallas_call x1, Pallas kernels: 89.9 us -> 75.3 us  [local(): pl.pallas_call(functools.partial(kernel, depth, rows), out_shape=jax.Shap...]
    unnamed x1, local copies, waits for them, and re-layouts: 2.19 us -> 0.8 us
where the time goes in v5:
time: 76.3 us; the launch traced here: 76.1 us
  Pallas kernels  75.3 us (99%)
  local copies, waits for them, and re-layouts  0.8 us (1%)
    pallas_call x1, Pallas kernels, local(): pl.pallas_call(functools.partial(kernel, depth, rows), out_shape=jax.Shap...  75.3 us

profile of v5, /device:TPU:0, one launch (start us, length us, event | category | flops | bytes accessed | tf_op | source)
XLA Modules:
  0.0 76.1 jit_solution(17606879004930600322)
XLA Ops:
  0.0 75.3 %shard_map.17 = f32[4,256,128]{2,1,0:T(8,128)S(1)} custom-call(f32[4,16,8,2048]{3,2,1,0:T(8,128)} %bitcast.3), custom_call_target="tpu_custom_call" | custom-call | tf_op jit(solution)/shard_map/pallas_call | solution.py:435
  75.3 0.8 %copy.4 = f32[4,128,1,256]{3,2,1,0:T(1,128)} copy(f32[4,128,1,256]{3,2,1,0:T(1,128)S(1)} %bitcast.2) | data formatting | bytes 1048576

commit v6 on v5

--- a/solution.py
+++ b/solution.py
@@ -370,7 +370,7 @@
         for ch in range(4):
             out_ref[ch, pl.ds(at, TILE, stride=parts), :] = value[ch]
 
-    @pl.loop(0, pieces + steps + 1)
+    @pl.loop(0, pieces + steps + 2)
     def _(i):
         @pl.when(i < pieces)
         def _():
@@ -399,15 +399,16 @@
                     last_copy(q).start()
                     put(x, q, held[steps][q, 0, x])
 
-    @pl.loop(0, pieces)
-    def _(q):
-        pair_copy(q)(lambda copy: copy.wait_send())
-        pl.when(has_next)(lambda: face_copy(0, q).wait_send())
-        pl.when(has_prev)(lambda: face_copy(1, q).wait_send())
-        for k in range(steps):
-            part_copy(k, q).wait_send()
-        last_copy(q).wait()
-        put(1 - x, q, final[q])
+        @pl.when(i >= steps + 2)
+        def _():
+            q = i - steps - 2
+            pair_copy(q)(lambda copy: copy.wait_send())
+            pl.when(has_next)(lambda: face_copy(0, q).wait_send())
+            pl.when(has_prev)(lambda: face_copy(1, q).wait_send())
+            for k in range(steps):
+                part_copy(k, q).wait_send()
+            last_copy(q).wait()
+            put(1 - x, q, final[q])
 
 
 def local(log_density):

time: 76.3 us -> 77.1 us (1.010)
  Pallas kernels: 75.3 us -> 76.2 us
    pallas_call x1, Pallas kernels: 75.3 us -> 76.2 us  [local(): pl.pallas_call(functools.partial(kernel, depth, rows), out_shape=jax.Shap...]
where the time goes in v6:
time: 77.1 us; the launch traced here: 77 us
  Pallas kernels  76.2 us (99%)
  local copies, waits for them, and re-layouts  0.8 us (1%)
    pallas_call x1, Pallas kernels, local(): pl.pallas_call(functools.partial(kernel, depth, rows), out_shape=jax.Shap...  76.2 us

profile of v6, /device:TPU:0, one launch (start us, length us, event | category | flops | bytes accessed | tf_op | source)
XLA Modules:
  0.0 77.0 jit_solution(2890319130040255747)
XLA Ops:
  0.0 76.2 %shard_map.17 = f32[4,256,128]{2,1,0:T(8,128)S(1)} custom-call(f32[4,16,8,2048]{3,2,1,0:T(8,128)} %bitcast.3), custom_call_target="tpu_custom_call" | custom-call | tf_op jit(solution)/shard_map/pallas_call | solution.py:436
  76.2 0.8 %copy.4 = f32[4,128,1,256]{3,2,1,0:T(1,128)} copy(f32[4,128,1,256]{3,2,1,0:T(1,128)S(1)} %bitcast.2) | data formatting | bytes 1048576

commit v7 on v5

--- a/solution.py
+++ b/solution.py
@@ -12,6 +12,7 @@
 TILE = 8
 LANES = 128
 BLOCK = 256
+SPAN = 512
 AHEAD = 2
 LOG2E = 1.4426950408889634
 
@@ -283,20 +284,20 @@
         t, begin = 1 + lax.rem(q, chunks), q // chunks * part
 
         def columns(b, carry):
-            base = pl.multiple_of(begin + b * BLOCK, BLOCK)
+            base = pl.multiple_of(begin + b * SPAN, SPAN)
 
             def lanes(v):
                 return pl.ds(pl.multiple_of(base + v * LANES, LANES), LANES)
 
             def load(s):
-                return [cells[s, t, :, lanes(v)] for v in range(BLOCK // LANES + 2)]
+                return [cells[s, t, :, lanes(v)] for v in range(SPAN // LANES + 2)]
 
             zero = jnp.zeros((TILE, LANES), jnp.float32)
-            sums = [[zero] * 4 for _ in range(BLOCK // LANES)]
+            sums = [[zero] * 4 for _ in range(SPAN // LANES)]
             before, here = load(0), load(1)
             for s in range(1, 2 * S + 1):
                 after = load(s + 1)
-                for v in range(BLOCK // LANES):
+                for v in range(SPAN // LANES):
                     both, swing, green, alpha = sums[v]
                     centre = here[v + 1]
                     left = pltpu.roll(jnp.where(is_right, here[v], centre), 1, 1)
@@ -317,15 +318,15 @@
                         alpha + weight,
                     ]
                 before, here = here, after
-            for v in range(BLOCK // LANES):
+            for v in range(SPAN // LANES):
                 both, swing, green, alpha = sums[v]
                 both, swing = (0.5 * 0.336) * both, (0.5 * 0.336) * swing
-                to = pl.ds(pl.multiple_of(b * BLOCK + v * LANES, LANES), LANES)
+                to = pl.ds(pl.multiple_of(b * SPAN + v * LANES, LANES), LANES)
                 for ch, value in enumerate((both + swing, 0.336 * green, both - swing, alpha)):
                     image[ch, :, to] = value
             return carry
 
-        lax.fori_loop(0, blocks, columns, 0)
+        lax.fori_loop(0, part // SPAN, columns, 0)
         turned = []
         for b in range(blocks):
             piece = image[:, :, b * BLOCK : (b + 1) * BLOCK].reshape(4 * TILE, BLOCK)
@@ -416,6 +417,7 @@
     groups = depth // 2
     fits = (
         4 <= depth <= LANES
+        and (LANES * depth) % SPAN == 0
         and depth & (depth - 1) == 0
         and W % (LANES * depth) == 0
         and R % (2 * TILE) == 0

time: 76.3 us -> 76.2 us (level)
  no operation moved by 1% of the time
where the time goes in v7:
time: 76.2 us; the launch traced here: 76 us
  Pallas kernels  75.2 us (99%)
  local copies, waits for them, and re-layouts  0.8 us (1%)
    pallas_call x1, Pallas kernels, local(): pl.pallas_call(functools.partial(kernel, depth, rows), out_shape=jax.Shap...  75.2 us

profile of v7, /device:TPU:0, one launch (start us, length us, event | category | flops | bytes accessed | tf_op | source)
XLA Modules:
  0.0 76.0 jit_solution(18270100733821490098)
XLA Ops:
  0.0 75.2 %shard_map.17 = f32[4,256,128]{2,1,0:T(8,128)S(1)} custom-call(f32[4,16,8,2048]{3,2,1,0:T(8,128)} %bitcast.3), custom_call_target="tpu_custom_call" | custom-call | tf_op jit(solution)/shard_map/pallas_call | solution.py:437
  75.2 0.8 %copy.4 = f32[4,128,1,256]{3,2,1,0:T(1,128)} copy(f32[4,128,1,256]{3,2,1,0:T(1,128)S(1)} %bitcast.2) | data formatting | bytes 1048576

commit v8 on v7

--- a/solution.py
+++ b/solution.py
@@ -143,7 +143,7 @@
         copy.start()
     pl.semaphore_wait(barrier, count)
 
-    def pair_copy(q):
+    def pair_copy(q, h):
         def apply(act):
             for g in range(parts):
                 low = g * part + (LANES if g else 0)
@@ -153,9 +153,9 @@
                 def _(g=g, low=low, high=high):
                     c = q - g * chunks
                     act(pltpu.make_async_remote_copy(
-                        src_ref=vol_ref.at[:, (1 - x) * chunks + c, :, pl.ds(low, high - low)],
-                        dst_ref=cells.at[pl.ds(mine, S), 1 + c, :, pl.ds(LANES + low, high - low)],
-                        send_sem=pair_send.at[q], recv_sem=pair_recv.at[q],
+                        src_ref=vol_ref.at[pl.ds(h * (S // 2), S // 2), (1 - x) * chunks + c, :, pl.ds(low, high - low)],
+                        dst_ref=cells.at[pl.ds(mine + h * (S // 2), S // 2), 1 + c, :, pl.ds(LANES + low, high - low)],
+                        send_sem=pair_send.at[h, q], recv_sem=pair_recv.at[h, q],
                         device_id=(partner, row), device_id_type=MESH,
                     ))
         return apply
@@ -209,7 +209,10 @@
             device_id=(partner, row), device_id_type=MESH,
         )
 
-    pl.loop(0, ahead)(lambda q: pair_copy(q)(start))
+    @pl.loop(0, ahead)
+    def _(q):
+        for h in range(2):
+            pair_copy(q, h)(start)
 
     has_next_row, has_prev_row = row <= rows - 2, row >= 1
     has_next, has_prev = z <= groups - 2, z >= 1
@@ -375,10 +378,11 @@
     def _(i):
         @pl.when(i < pieces)
         def _():
-            pair_copy(i)(lambda copy: copy.wait_recv())
-            pl.when(i + ahead < pieces)(lambda: pair_copy(i + ahead)(start))
+            for h in range(2):
+                pair_copy(i, h)(lambda copy: copy.wait_recv())
             pl.when(has_next)(lambda: face_copy(0, i).start())
             pl.when(has_prev)(lambda: face_copy(1, i).start())
+            pl.when(i + ahead < pieces)(lambda: pair_copy(i + ahead, 0)(start))
 
         @pl.when(jnp.logical_and(i >= 1, i <= pieces))
         def _():
@@ -388,6 +392,7 @@
             shade(q)
             part_copy(0, q).start()
 
+        pl.when(i + ahead < pieces)(lambda: pair_copy(i + ahead, 1)(start))
         for k in range(steps):
 
             @pl.when(jnp.logical_and(i >= k + 2, i <= pieces + k + 1))
@@ -402,7 +407,8 @@
 
     @pl.loop(0, pieces)
     def _(q):
-        pair_copy(q)(lambda copy: copy.wait_send())
+        for h in range(2):
+            pair_copy(q, h)(lambda copy: copy.wait_send())
         pl.when(has_next)(lambda: face_copy(0, q).wait_send())
         pl.when(has_prev)(lambda: face_copy(1, q).wait_send())
         for k in range(steps):
@@ -421,6 +427,7 @@
         and depth & (depth - 1) == 0
         and W % (LANES * depth) == 0
         and R % (2 * TILE) == 0
+        and S % 2 == 0
     )
     if not fits:
         return local_general(log_density)
@@ -450,7 +457,7 @@
             *partial,
             *arrivals,
             DMA, DMA((2,)), DMA,
-            DMA((pieces,)), DMA((pieces,)),
+            DMA((2, pieces)), DMA((2, pieces)),
             DMA, DMA,
             DMA((2,)), DMA((2,)),
             DMA((2, pieces)), DMA((2, pieces)),

time: 76.2 us -> 76.7 us (level)
  no operation moved by 1% of the time
where the time goes in v8:
time: 76.7 us; the launch traced here: 76.6 us
  Pallas kernels  75.7 us (99%)
  local copies, waits for them, and re-layouts  0.8 us (1%)
    pallas_call x1, Pallas kernels, local(): pl.pallas_call(functools.partial(kernel, depth, rows), out_shape=jax.Shap...  75.7 us

profile of v8, /device:TPU:0, one launch (start us, length us, event | category | flops | bytes accessed | tf_op | source)
XLA Modules:
  0.0 76.6 jit_solution(1436164014003093156)
XLA Ops:
  0.0 75.7 %shard_map.17 = f32[4,256,128]{2,1,0:T(8,128)S(1)} custom-call(f32[4,16,8,2048]{3,2,1,0:T(8,128)} %bitcast.3), custom_call_target="tpu_custom_call" | custom-call | tf_op jit(solution)/shard_map/pallas_call | solution.py:444
  75.8 0.8 %copy.4 = f32[4,128,1,256]{3,2,1,0:T(1,128)} copy(f32[4,128,1,256]{3,2,1,0:T(1,128)S(1)} %bitcast.2) | data formatting | bytes 1048576

commit v9 on v7

--- a/solution.py
+++ b/solution.py
@@ -95,7 +95,6 @@
     part = LANES * depth
     parts = W // part
     pieces = parts * chunks
-    ahead = min(AHEAD, pieces)
     span = pl.ds(LANES, W)
     log_extinction = math.log2(0.5 / (S * depth) * LOG2E)
 
@@ -106,6 +105,7 @@
     me, row = lax.axis_index("depth"), lax.axis_index("rows")
     x, z = lax.rem(me, 2), me // 2
     first = me - x
+    ahead = jnp.minimum(AHEAD + 1 - lax.rem(row, 2), pieces)
     partner = first + 1 - x
     mine = 1 + S * x
 

time: 76.2 us -> 77.2 us (1.013)
  Pallas kernels: 75.2 us -> 76.3 us
    pallas_call x1, Pallas kernels: 75.2 us -> 76.3 us  [local(): pl.pallas_call(functools.partial(kernel, depth, rows), out_shape=jax.Shap...]
where the time goes in v9:
time: 77.2 us; the launch traced here: 77.1 us
  Pallas kernels  76.3 us (99%)
  local copies, waits for them, and re-layouts  0.8 us (1%)
    pallas_call x1, Pallas kernels, local(): pl.pallas_call(functools.partial(kernel, depth, rows), out_shape=jax.Shap...  76.3 us

profile of v9, /device:TPU:0, one launch (start us, length us, event | category | flops | bytes accessed | tf_op | source)
XLA Modules:
  0.0 77.1 jit_solution(14003873765226060594)
XLA Ops:
  0.0 76.3 %shard_map.17 = f32[4,256,128]{2,1,0:T(8,128)S(1)} custom-call(f32[4,16,8,2048]{3,2,1,0:T(8,128)} %bitcast.3), custom_call_target="tpu_custom_call" | custom-call | tf_op jit(solution)/shard_map/pallas_call | solution.py:437
  76.3 0.8 %copy.4 = f32[4,128,1,256]{3,2,1,0:T(1,128)} copy(f32[4,128,1,256]{3,2,1,0:T(1,128)S(1)} %bitcast.2) | data formatting | bytes 1048576

commit v10 on v7

--- a/solution.py
+++ b/solution.py
@@ -14,6 +14,7 @@
 BLOCK = 256
 SPAN = 512
 AHEAD = 2
+LAG = 2
 LOG2E = 1.4426950408889634
 
 
@@ -371,7 +372,7 @@
         for ch in range(4):
             out_ref[ch, pl.ds(at, TILE, stride=parts), :] = value[ch]
 
-    @pl.loop(0, pieces + steps + 1)
+    @pl.loop(0, pieces + LAG * steps + 1)
     def _(i):
         @pl.when(i < pieces)
         def _():
@@ -390,9 +391,9 @@
 
         for k in range(steps):
 
-            @pl.when(jnp.logical_and(i >= k + 2, i <= pieces + k + 1))
+            @pl.when(jnp.logical_and(i >= 1 + LAG * (k + 1), i <= pieces + LAG * (k + 1)))
             def _(k=k):
-                q = i - 2 - k
+                q = i - 1 - LAG * (k + 1)
                 combine(k, q)
                 if k + 1 < steps:
                     part_copy(k + 1, q).start()

time: 76.2 us -> 74.8 us (0.982)
  Pallas kernels: 75.2 us -> 73.9 us
    pallas_call x1, Pallas kernels: 75.2 us -> 73.9 us  [local(): pl.pallas_call(functools.partial(kernel, depth, rows), out_shape=jax.Shap...]
where the time goes in v10:
time: 74.8 us; the launch traced here: 74.7 us
  Pallas kernels  73.9 us (99%)
  local copies, waits for them, and re-layouts  0.8 us (1%)
    pallas_call x1, Pallas kernels, local(): pl.pallas_call(functools.partial(kernel, depth, rows), out_shape=jax.Shap...  73.9 us

profile of v10, /device:TPU:0, one launch (start us, length us, event | category | flops | bytes accessed | tf_op | source)
XLA Modules:
  0.0 74.7 jit_solution(2648963420216389834)
XLA Ops:
  0.0 73.9 %shard_map.17 = f32[4,256,128]{2,1,0:T(8,128)S(1)} custom-call(f32[4,16,8,2048]{3,2,1,0:T(8,128)} %bitcast.3), custom_call_target="tpu_custom_call" | custom-call | tf_op jit(solution)/shard_map/pallas_call | solution.py:438
  73.9 0.8 %copy.4 = f32[4,128,1,256]{3,2,1,0:T(1,128)} copy(f32[4,128,1,256]{3,2,1,0:T(1,128)S(1)} %bitcast.2) | data formatting | bytes 1048576

commit v11 on v10

--- a/solution.py
+++ b/solution.py
@@ -13,7 +13,7 @@
 LANES = 128
 BLOCK = 256
 SPAN = 512
-AHEAD = 2
+AHEAD = 1
 LAG = 2
 LOG2E = 1.4426950408889634
 

time: 74.8 us -> 98.7 us (1.32)
  Pallas kernels: 73.9 us -> 97.7 us
    pallas_call x1, Pallas kernels: 73.9 us -> 97.7 us  [local(): pl.pallas_call(functools.partial(kernel, depth, rows), out_shape=jax.Shap...]
where the time goes in v11:
time: 98.7 us; the launch traced here: 98.5 us
  Pallas kernels  97.7 us (99%)
    pallas_call x1, Pallas kernels, local(): pl.pallas_call(functools.partial(kernel, depth, rows), out_shape=jax.Shap...  97.7 us

profile of v11, /device:TPU:0, one launch (start us, length us, event | category | flops | bytes accessed | tf_op | source)
XLA Modules:
  0.0 98.5 jit_solution(1848394171120339998)
XLA Ops:
  0.0 97.7 %shard_map.17 = f32[4,256,128]{2,1,0:T(8,128)S(1)} custom-call(f32[4,16,8,2048]{3,2,1,0:T(8,128)} %bitcast.3), custom_call_target="tpu_custom_call" | custom-call | tf_op jit(solution)/shard_map/pallas_call | solution.py:438
  97.8 0.8 copy.4
